TPU v7x, 32 devices: a whole 2x2x4 slice. The times are simulated.
32 devices in a mesh: clip: 4 (over y, x), tm: 8 (over z, core).
Axes of the slice: x: 2, y: 2, z: 4, core: 2. Of those that a mesh axis runs over, the one named last changes fastest.
Arguments:
- clip_in: bfloat16 [8, 32, 14, 14, 1024], P('clip', 'tm'), may hold values from -6 to 6
- cotangent: bfloat16 [8, 16, 7, 7, 2048], P('clip', 'tm'), may hold values from -6 to 6
- frame_count: int32 [8], replicated, may hold values from 2 to 4, as said below
- clip_count: int32 [4], P('clip'), may hold values from 1 to 2, as said below
- narrow_a: bfloat16 [1024, 256], replicated, may hold values from -0.1875 to 0.1875
- narrow_gain_a: float32 [256], replicated, may hold values from 0.5 to 1.5
- narrow_bias_a: float32 [256], replicated, may hold values from -0.5 to 0.5
- mixing_a: bfloat16 [256, 256], replicated, may hold values from -0.375 to 0.375
- depthwise_a: bfloat16 [256, 27], replicated, may hold values from -1.25 to 1.25
- depth_gain_a: float32 [256], replicated, may hold values from 0.5 to 1.5
- depth_bias_a: float32 [256], replicated, may hold values from -0.5 to 0.5
- widen_a: bfloat16 [256, 1024], replicated, may hold values from -0.375 to 0.375
- widen_gain_a: float32 [1024], replicated, may hold values from 0.5 to 1.5
- widen_bias_a: float32 [1024], replicated, may hold values from -0.5 to 0.5
- narrow_b: bfloat16 [1024, 512], replicated, may hold values from -0.1875 to 0.1875
- narrow_gain_b: float32 [512], replicated, may hold values from 0.5 to 1.5
- narrow_bias_b: float32 [512], replicated, may hold values from -0.5 to 0.5
- mixing_b: bfloat16 [512, 512], replicated, may hold values from -0.25 to 0.25
- depthwise_b: bfloat16 [512, 27], replicated, may hold values from -1.25 to 1.25
- depth_gain_b: float32 [512], replicated, may hold values from 0.5 to 1.5
- depth_bias_b: float32 [512], replicated, may hold values from -0.5 to 0.5
- widen_b: bfloat16 [512, 2048], replicated, may hold values from -0.25 to 0.25
- widen_gain_b: float32 [2048], replicated, may hold values from 0.5 to 1.5
- widen_bias_b: float32 [2048], replicated, may hold values from -0.5 to 0.5
- shortcut_b: bfloat16 [1024, 2048], replicated, may hold values from -0.1875 to 0.1875
- shortcut_gain_b: float32 [2048], replicated, may hold values from 0.5 to 1.5
- shortcut_bias_b: float32 [2048], replicated, may hold values from -0.5 to 0.5
Outputs:
- block_out: bfloat16 [8, 16, 7, 7, 2048], P('clip', 'tm')
- input_grad: bfloat16 [8, 32, 14, 14, 1024], P('clip', 'tm')
- grad_narrow_a: float32 [1024, 256], P('tm')
- grad_narrow_gain_a: float32 [256], replicated
- grad_narrow_bias_a: float32 [256], replicated
- grad_mixing_a: float32 [256, 256], P('tm')
- grad_depthwise_a: float32 [256, 27], P('tm')
- grad_depth_gain_a: float32 [256], replicated
- grad_depth_bias_a: float32 [256], replicated
- grad_widen_a: float32 [256, 1024], P('tm')
- grad_widen_gain_a: float32 [1024], replicated
- grad_widen_bias_a: float32 [1024], replicated
- grad_narrow_b: float32 [1024, 512], P('tm')
- grad_narrow_gain_b: float32 [512], replicated
- grad_narrow_bias_b: float32 [512], replicated
- grad_mixing_b: float32 [512, 512], P('tm')
- grad_depthwise_b: float32 [512, 27], P('tm')
- grad_depth_gain_b: float32 [512], replicated
- grad_depth_bias_b: float32 [512], replicated
- grad_widen_b: float32 [512, 2048], P('tm')
- grad_widen_gain_b: float32 [2048], replicated
- grad_widen_bias_b: float32 [2048], replicated
- grad_shortcut_b: float32 [1024, 2048], P('tm')
- grad_shortcut_gain_b: float32 [2048], replicated
- grad_shortcut_bias_b: float32 [2048], replicated
Inputs may be any that keep to these rules, and one draw needn't show every extreme that they name: Index i of tm holds frame_count[i] consecutive frames of every clip, in order of i; the counts of indices 2 k and 2 k + 1 sum to 6; some index holds exactly 4 in every draw. Clip slots 0 .. clip_count[k] - 1 of clip index k are live; some index has all 2 live in every draw.
All inputs are finite; a program needn't handle non-finite values.
Results may differ from a plain program's by a relative error of at most 0.02.
Values may be sent and summed in bfloat16 or wider, within the bound.
A program may use at most 384 MiB of HBM per device.

v0:
```python
import functools

import jax
import jax.numpy as jnp
from jax import lax
from jax.experimental import pallas as pl
from jax.experimental.pallas import tpu as pltpu
from jax.sharding import PartitionSpec as P

epsilon = 1e-05
LANES = 128
MESH = pl.DeviceIdType.MESH
F32 = jnp.float32
BF16 = jnp.bfloat16

NORMS = ("na", "da", "wa", "nb", "db", "wb", "sb")


HALO = (("dva", "dva"), ("hs2", "hr2"), ("dz2", "hr3"), ("hs2", "hr2"))


class Refs:
    pass


def logistic(z):
    return 0.5 * jnp.tanh(0.5 * z) + 0.5


def silu(z):
    return z * logistic(z)


def slope(z):
    q = logistic(z)
    return q * (1.0 + z * (1.0 - q))


def dot(x, w):
    return jnp.dot(x, w, preferred_element_type=F32)


def dot_bt(x, w):
    return lax.dot_general(x, w, (((1,), (1,)), ((), ())), preferred_element_type=F32)


def dot_at(x, y):
    return lax.dot_general(x, y, (((0,), (0,)), ((), ())), preferred_element_type=F32)


def rows8(v):
    return jnp.sum(v.reshape(v.shape[0] // 8, 8, v.shape[1]), axis=0)


def tile_lanes(v, width):
    if width == v.shape[1]:
        return v
    return jnp.concatenate([v] * (width // v.shape[1]), axis=1)


class Dims:
    def __init__(self, mesh, clip_in, cotangent, ca, cb):
        self.nc = mesh.shape["clip"]
        self.nt = mesh.shape["tm"]
        self.phases = [("tm", 1, self.nt)] if self.nt <= 8 else [("tm", 1, 8), ("tm", 8, self.nt // 8)]
        self.phases.append(("clip", 1, self.nc))
        self.n, self.t, self.h, self.w, self.c0 = clip_in
        self.ca, self.cb = ca, cb
        self.co = cotangent[-1]
        self.wp = -(-(self.w + 1) // 16) * 16
        self.f = self.n * self.t
        self.fr = self.h * self.wp
        self.er = (self.h + 2) * self.wp
        self.slots = self.t + 2
        self.t2, self.h2, self.w2 = self.t // 2, self.h // 2, self.w // 2
        self.wh = self.wp // 2
        self.f2 = self.n * self.t2
        self.hr = self.h2 * self.wh
        self.r2 = self.f2 * self.hr
        self.ur = (self.h2 + 1) * self.wp


def messages(d):
    return dict(
        na=(3, d.ca), da=(2, d.ca), wa=(2, d.c0), nb=(2, d.cb), sk=(2, d.co), db=(2, d.cb),
        wb=(2, d.co), gz=(3, d.co), gdb=(2, d.cb), gnb=(2, d.cb), gwa=(2, d.c0), gda=(2, d.ca),
        gna=(2, d.ca),
    )


def scratch_of(d):
    V = pltpu.VMEM
    DM = pltpu.SemaphoreType.DMA
    s = dict(
        raw=V((2, d.h, d.w, d.c0), BF16),
        x=V((d.f, d.h, d.wp, d.c0), BF16),
        a1=V((d.f, d.fr, d.ca), F32),
        h1=V((d.f, d.fr, d.ca), BF16),
        v1=V((d.n * d.slots, d.er, d.ca), BF16),
        d1=V((d.f, d.fr, d.ca), F32),
        h2=V((d.f, d.fr, d.ca), BF16),
        a3=V((d.f, d.fr, d.c0), BF16),
        y1=V((d.f, d.fr, d.c0), BF16),
        b1=V((d.f, d.fr, d.cb), F32),
        g1=V((d.f, d.fr, d.cb), BF16),
        v2=V((d.n * d.slots, d.er, d.cb), BF16),
        d2=V((d.f2, d.hr, d.cb), F32),
        g2=V((d.r2, d.cb), BF16),
        e=V((d.f2, d.hr, d.c0), F32),
        eb=V((d.r2, d.c0), BF16),
        b3s=V((2 * (d.co // d.cb), d.r2, d.cb), F32),
        dz2=V((d.co // d.cb, d.r2, d.cb), F32),
        db3=V((d.r2, d.co), BF16),
        ds=V((d.r2, d.co), BF16),
        u=V((d.n * d.slots, d.er, d.ca), F32),
        dvb=V((d.f, d.fr, d.cb), BF16),
        dz1=V((d.f, d.fr, d.c0), BF16),
        dva=V((max(d.f, 4 * d.n), d.fr, d.ca), BF16),
        cot=V((d.n, d.t2, d.h2, d.w2, d.co), BF16),
        acc=V((3, 8, d.co), F32),
        inv=V((1, d.co), F32),
        kta=V((32, d.ca), F32),
        ktb=V((32, d.cb), F32),
        vec=V((16, d.co), F32),
        gka=V((32, d.ca), F32),
        gkb=V((32, d.cb), F32),
        par=V((len(NORMS), 8, d.co), F32),
        hs2=V((2, d.n, d.fr, d.cb), BF16),
        hr2=V((2, d.n, d.fr, d.cb), BF16),
        hr3=V((2, 2, d.n * d.hr, d.cb), F32),
        hsend=DM((4, 2)),
        hrecv=DM((4, 2)),
        w_na=V((d.c0, d.ca), BF16),
        w_ma=V((d.ca, d.ca), BF16),
        w_wa=V((d.ca, d.c0), BF16),
        w_nb=V((d.c0, d.cb), BF16),
        w_mb=V((d.cb, d.cb), BF16),
        w_wb=V((d.cb, d.co), BF16),
        w_sb=V((d.c0, d.co), BF16),
        small=V((16, d.co), F32),
        wsem=DM((16,)),
        xsem=DM((2,)),
        osem=DM((16,)),
        isem=DM((2,)),
    )
    for name, (k, c) in messages(d).items():
        for p, (_, _, size) in enumerate(d.phases):
            s[f"ms{p}_{name}"] = V((k, c), F32)
            s[f"ml{p}_{name}"] = V((size, k, c), F32)
        s["mq_" + name] = DM((len(d.phases), 2))
    return s


INPUTS = (
    "clip_in", "cotangent", "frame_count", "clip_count", "i_na", "i_ma", "i_wa", "i_nb", "i_mb",
    "i_wb", "i_sb", "i_kta", "i_ktb", "i_vec",
)
OUTPUTS = (
    "block_out", "input_grad", "o_small", "o_gka", "o_gkb", "o_na", "o_ma", "o_wa", "o_nb", "o_mb",
    "o_wb", "o_sb",
)
WEIGHTS = ("na", "ma", "wa", "nb", "mb", "wb", "sb")


def kernel(d, names, *refs):
    r = Refs()
    for name, ref in zip(names, refs):
        setattr(r, name, ref)
    clip = lax.axis_index("clip")
    tm = lax.axis_index("tm")
    msgs = messages(d)

    def weight_copy(i):
        name = WEIGHTS[i]
        return pltpu.make_async_copy(
            getattr(r, "i_" + name), getattr(r, "w_" + name), r.wsem.at[i]
        )

    def frame_copy(f, slot):
        return pltpu.make_async_copy(r.clip_in.at[f // d.t, f % d.t], r.raw.at[slot], r.xsem.at[slot])

    frame_copy(0, 0).start()
    weight_copy(0).start()
    frame_copy(1, 1).start()
    for i, (src, dst) in enumerate(
        ((r.i_kta, r.kta), (r.i_ktb, r.ktb), (r.i_vec, r.vec), (r.cotangent, r.cot))
    ):
        pltpu.make_async_copy(src, dst, r.wsem.at[8 + i]).start()
    for i in range(1, len(WEIGHTS)):
        weight_copy(i).start()

    barrier = pltpu.get_barrier_semaphore()

    def place(p):
        axis, stride, size = d.phases[p]
        return lax.rem((clip if axis == "clip" else tm) // stride, size)

    def peer(p, k):
        axis, stride, size = d.phases[p]
        shift = (lax.rem(place(p) + k, size) - place(p)) * stride
        return (clip + shift, tm) if axis == "clip" else (clip, tm + shift)

    for p in range(len(d.phases)):
        @pl.loop(1, d.phases[p][2])
        def _(k):
            pl.semaphore_signal(barrier, 1, device_id=peer(p, k), device_id_type=MESH)

    frames = jnp.clip(r.frame_count[tm], 2, d.t)
    start = lax.fori_loop(
        0, d.nt, lambda i, s: s + jnp.where(i < tm, r.frame_count[i], 0), jnp.int32(0)
    )
    parity = start & 1
    out_frames = jnp.clip((frames + 1 - parity) // 2, 1, d.t2)
    live = r.clip_count[0]

    def one(cond):
        return jnp.where(cond, 1.0, 0.0).astype(F32)

    def mask_f(f):
        return one((lax.rem(f, d.t) < frames) & (f // d.t < live))

    def mask_o(i):
        return one((lax.rem(i, d.t2) < out_frames) & (i // d.t2 < live))

    has_prev = one(tm > 0)
    has_next = one(tm < d.nt - 1)

    full_cols = one(lax.rem(lax.broadcasted_iota(jnp.int32, (d.fr, LANES), 0), d.wp) < d.w)
    half_cols = one(lax.rem(lax.broadcasted_iota(jnp.int32, (d.hr, LANES), 0), d.wh) < d.w2)
    row_cols = one(lax.broadcasted_iota(jnp.int32, (d.wp, LANES), 0) < d.w)

    last = len(d.phases) - 1

    def ar_send(name, p, value):
        src, slots = getattr(r, f"ms{p}_{name}"), getattr(r, f"ml{p}_{name}")
        q = getattr(r, "mq_" + name)
        src[...] = value

        @pl.loop(1, d.phases[p][2])
        def _(k):
            pltpu.make_async_remote_copy(
                src, slots.at[place(p)], q.at[p, 0], q.at[p, 1], device_id=peer(p, k),
                device_id_type=MESH,
            ).start()

        slots[place(p)] = value

    def ar_wait(name, p, which):
        part = getattr(r, f"ml{p}_{name}").at[pl.ds(0, d.phases[p][2] - 1)]
        pltpu.make_async_copy(part, part, getattr(r, "mq_" + name).at[p, which]).wait()

    def ar_total(name, p):
        ar_wait(name, p, 1)
        return jnp.sum(getattr(r, f"ml{p}_{name}")[...], axis=0)

    def ar_start(name, rows):
        ar_send(name, 0, jnp.concatenate(rows, axis=0))

    def ar_mid(name):
        for p in range(last):
            ar_send(name, p + 1, ar_total(name, p))

    def ar_end(name):
        total = ar_total(name, last)
        return [total[i : i + 1, :] for i in range(msgs[name][0])]

    def ar_drain(name):
        for p in range(last + 1):
            ar_wait(name, p, 0)

    def halo_source(i, side):
        src = getattr(r, HALO[i][0])
        if HALO[i][0] == "dz2":
            return src.at[2 * side : 2 * side + 2, d.r2 // 2 :, :]
        if HALO[i][0] == "dva":
            return src.at[side * d.n : (side + 1) * d.n]
        return src.at[side]

    def halo_target(i, side):
        dst = getattr(r, HALO[i][1])
        if HALO[i][1] == "dva":
            return dst.at[(2 + side) * d.n : (3 + side) * d.n]
        return dst.at[side]

    def halo_copy(i, side):
        return pltpu.make_async_remote_copy(
            halo_source(i, side), halo_target(i, 1 - side), r.hsend.at[i, side], r.hrecv.at[i, 1 - side],
            device_id=(clip, tm + (2 * side - 1)), device_id_type=MESH,
        )

    def halo_start(i):
        @pl.when(tm > 0)
        def _():
            halo_copy(i, 0).start()

        @pl.when(tm < d.nt - 1)
        def _():
            halo_copy(i, 1).start()

    def halo_wait(i):
        lower, upper = halo_target(i, 0), halo_target(i, 1)

        @pl.when(tm > 0)
        def _():
            pltpu.make_async_copy(lower, lower, r.hrecv.at[i, 0]).wait()

        @pl.when(tm < d.nt - 1)
        def _():
            pltpu.make_async_copy(upper, upper, r.hrecv.at[i, 1]).wait()

        @pl.when(tm == 0)
        def _():
            lower[...] = jnp.zeros(lower.shape, lower.dtype)

        @pl.when(tm == d.nt - 1)
        def _():
            upper[...] = jnp.zeros(upper.shape, upper.dtype)

    def halo_drain(i):
        @pl.when(tm > 0)
        def _():
            pltpu.make_async_copy(
                halo_source(i, 0), halo_source(i, 0), r.hsend.at[i, 0]
            ).wait()

        @pl.when(tm < d.nt - 1)
        def _():
            pltpu.make_async_copy(
                halo_source(i, 1), halo_source(i, 1), r.hsend.at[i, 1]
            ).wait()

    order = {name: i for i, name in enumerate(NORMS)}
    width = dict(na=d.ca, da=d.ca, wa=d.c0, nb=d.cb, db=d.cb, wb=d.co, sb=d.co)

    def norm_set(name, sums, scale):
        i, c = order[name], width[name]
        inv = r.inv[:, :c] * scale
        mu = sums[0] * inv
        rs = lax.rsqrt(sums[1] * inv - mu * mu + epsilon)
        s = r.vec[2 * i : 2 * i + 1, :c] * rs
        r.par[i, 0:1, :c] = s
        r.par[i, 1:2, :c] = r.vec[2 * i + 1 : 2 * i + 2, :c] - mu * s
        r.par[i, 2:3, :c] = rs
        r.par[i, 3:4, :c] = mu

    def norm_of(name, lo, hi):
        i = order[name]
        return r.par[i, 0:1, lo:hi], r.par[i, 1:2, lo:hi]

    def back_set(name, sum_one, sum_two, scale):
        i, c = order[name], width[name]
        inv = r.inv[:, :c] * scale
        s, rs, mu = r.par[i, 0:1, :c], r.par[i, 2:3, :c], r.par[i, 3:4, :c]
        dgain = rs * (sum_two - mu * sum_one)
        gamma = s * rs * dgain * inv
        r.par[i, 4:5, :c] = s * sum_one * inv - gamma * mu
        r.par[i, 5:6, :c] = gamma
        r.small[2 * i : 2 * i + 1, :c] = dgain
        r.small[2 * i + 1 : 2 * i + 2, :c] = sum_one

    def back_of(name, lo, hi):
        i = order[name]
        return r.par[i, 0:1, lo:hi], r.par[i, 4:5, lo:hi], r.par[i, 5:6, lo:hi]

    def acc_clear(k, c):
        for i in range(k):
            r.acc[i, :, :c] = jnp.zeros((8, c), F32)

    def acc_rows(k, c):
        return [jnp.sum(r.acc[i, :, :c], axis=0, keepdims=True) for i in range(k)]

    def lanes(c, step=LANES):
        return [(lo, lo + step) for lo in range(0, c, step)]

    def slot_of(f):
        n = f // d.t
        return n * d.slots + 1 + (f - n * d.t)

    acc_clear(2, d.ca)
    weight_copy(0).wait()

    @pl.loop(0, d.f)
    def _(f):
        slot = lax.rem(f, 2)
        frame_copy(f, slot).wait()
        r.x[f] = jnp.zeros((d.h, d.wp, d.c0), BF16)
        r.x[f, :, 0 : d.w, :] = r.raw[slot]

        @pl.when(f + 2 < d.f)
        def _():
            frame_copy(f + 2, slot).start()

        v = dot(r.x[f].reshape(d.fr, d.c0), r.w_na[...])
        r.a1[f] = v
        m = mask_f(f)
        r.acc[0, :, : d.ca] += rows8(v) * m
        r.acc[1, :, : d.ca] += rows8(v * v) * m

    for n in range(d.n):
        r.dva[n] = r.a1[n * d.t].astype(BF16)
        r.dva[d.n + n] = r.a1[n * d.t + frames - 1].astype(BF16)
    pl.semaphore_wait(barrier, sum(size - 1 for _, _, size in d.phases))
    cells = (jnp.minimum(live, d.n) * frames * (d.h * d.w)).astype(F32)
    ar_start("na", acc_rows(2, d.ca) + [jnp.full((1, d.ca), 1.0, F32) * cells])
    halo_start(0)
    for i in range(3):
        src, dst = ((r.i_kta, r.kta), (r.i_ktb, r.ktb), (r.i_vec, r.vec))[i]
        pltpu.make_async_copy(src, dst, r.wsem.at[8 + i]).wait()
    for ref in (r.v1, r.v2):
        @pl.loop(0, d.n * d.slots)
        def _(i):
            zero = jnp.zeros((d.wp, ref.shape[2]), ref.dtype)
            ref[i, 0 : d.wp, :] = zero
            ref[i, d.er - d.wp : d.er, :] = zero
    weight_copy(1).wait()
    ar_mid("na")
    sums = ar_end("na")
    inv_cells = 1.0 / sums[2]
    for lo, hi in lanes(d.co, d.ca):
        r.inv[:, lo:hi] = inv_cells
    norm_set("na", sums, 1.0)

    half = float((d.h * d.w * 2) // (d.h2 * d.w2))

    def activated(v, name, lo, hi, cols, m):
        s, b = norm_of(name, lo, hi)
        return silu(v * s + b) * (cols * m)

    def mixed(hidden, weight):
        return dot(hidden, weight).astype(BF16)

    def inner(ref_in, hid, framed, name, weight, c, half_i):
        cols = full_cols

        @pl.loop(0, d.f)
        def _(f):
            m = mask_f(f)
            for lo, hi in lanes(c):
                hid[f, :, lo:hi] = activated(ref_in[f, :, lo:hi], name, lo, hi, cols, m).astype(BF16)
            framed[slot_of(f), d.wp : d.wp + d.fr, :] = mixed(hid[f], weight[...]).astype(framed.dtype)

        halo_wait(half_i)
        sides = (halo_target(half_i, 0), halo_target(half_i, 1))
        for n in range(d.n):
            for side in range(2):
                m = (has_prev, has_next)[side] * one(n < live)
                h = jnp.concatenate(
                    [
                        activated(sides[side][n, :, lo:hi].astype(F32), name, lo, hi, cols, m).astype(BF16)
                        for lo, hi in lanes(c)
                    ],
                    axis=1,
                )
                v = mixed(h, weight[...])
                if side == 0:
                    framed[n * d.slots, d.wp : d.wp + d.fr, :] = v.astype(framed.dtype)
                else:
                    for k in range(1, d.t):
                        at = (n * d.slots + 1 + k, slice(d.wp, d.wp + d.fr), slice(None))
                        framed[at] = (framed[at].astype(F32) + v.astype(F32) * one(frames == k)).astype(
                            framed.dtype
                        )
                    framed[n * d.slots + 1 + d.t, d.wp : d.wp + d.fr, :] = v.astype(framed.dtype)

    inner(r.a1, r.h1, r.v1, "na", r.w_ma, d.ca, 0)

    def taps(ref, lo):
        return [ref[i : i + 1, lo : lo + LANES] for i in range(27)]

    acc_clear(2, d.ca)

    @pl.loop(0, d.f)
    def _(f):
        base = slot_of(f) - 1
        m = mask_f(f)
        for lo, hi in lanes(d.ca):
            k = taps(r.kta, lo)
            one_sum = jnp.zeros((8, LANES), F32)
            two_sum = jnp.zeros((8, LANES), F32)
            for h in range(d.h):
                parts = [None] * 3
                for a in range(3):
                    for b in range(3):
                        v = r.v1[base + a, (h + b) * d.wp : (h + b + 1) * d.wp, lo:hi].astype(F32)
                        for e in range(3):
                            p = v * k[9 * a + 3 * b + e]
                            parts[e] = p if parts[e] is None else parts[e] + p
                o = parts[1] + pltpu.roll(parts[0], 1, 0) + pltpu.roll(parts[2], d.wp - 1, 0)
                o = o * row_cols
                r.d1[f, h * d.wp : (h + 1) * d.wp, lo:hi] = o
                one_sum += rows8(o)
                two_sum += rows8(o * o)
            r.acc[0, :, lo:hi] += one_sum * m
            r.acc[1, :, lo:hi] += two_sum * m

    ar_start("da", acc_rows(2, d.ca))
    weight_copy(2).wait()
    ar_mid("da")
    norm_set("da", ar_end("da"), 1.0)

    acc_clear(2, d.c0)

    @pl.loop(0, d.f)
    def _(f):
        m = mask_f(f)
        for lo, hi in lanes(d.ca):
            r.h2[f, :, lo:hi] = activated(r.d1[f, :, lo:hi], "da", lo, hi, full_cols, m).astype(BF16)
        for lo, hi in lanes(d.c0, 256):
            v = dot(r.h2[f], r.w_wa[:, lo:hi])
            r.a3[f, :, lo:hi] = v.astype(BF16)
            r.acc[0, :, lo:hi] += rows8(v)
            r.acc[1, :, lo:hi] += rows8(v * v)

    ar_start("wa", acc_rows(2, d.c0))
    weight_copy(3).wait()
    ar_mid("wa")
    norm_set("wa", ar_end("wa"), 1.0)

    def joined(f, lo, hi):
        s, b = norm_of("wa", lo, hi)
        x = r.x[f, :, :, lo:hi].reshape(d.fr, hi - lo).astype(F32)
        return r.a3[f, :, lo:hi].astype(F32) * s + b + x

    acc_clear(2, d.cb)

    @pl.loop(0, d.f)
    def _(f):
        m = mask_f(f)
        for lo, hi in lanes(d.c0):
            r.y1[f, :, lo:hi] = (silu(joined(f, lo, hi)) * (full_cols * m)).astype(BF16)
        for lo, hi in lanes(d.cb, 256):
            v = dot(r.y1[f], r.w_nb[:, lo:hi])
            r.b1[f, :, lo:hi] = v
            r.acc[0, :, lo:hi] += rows8(v)
            r.acc[1, :, lo:hi] += rows8(v * v)

    for n in range(d.n):
        r.hs2[0, n] = r.b1[n * d.t].astype(BF16)
        r.hs2[1, n] = r.b1[n * d.t + frames - 1].astype(BF16)
    ar_start("nb", acc_rows(2, d.cb))
    halo_start(1)

    rows_e = lax.broadcasted_iota(jnp.int32, (d.hr, d.fr), 0)
    cols_e = lax.broadcasted_iota(jnp.int32, (d.hr, d.fr), 1)
    pick = one(
        (cols_e == (rows_e // d.wh) * (2 * d.wp) + lax.rem(rows_e, d.wh) * 2)
    ).astype(BF16)

    @pl.loop(0, d.f2)
    def _(i):
        n = i // d.t2
        f = n * d.t + parity + 2 * (i - n * d.t2)
        for lo, hi in lanes(d.c0, 512):
            r.e[i, :, lo:hi] = dot(pick, r.y1[f, :, lo:hi])

    r.eb[...] = r.e[...].reshape(d.r2, d.c0).astype(BF16)
    weight_copy(6).wait()
    acc_clear(2, d.co)

    @pl.loop(0, d.co // d.cb)
    def _(j):
        for half_lo in range(0, d.cb, 256):
            at = pl.ds(pl.multiple_of(j * d.cb + half_lo, 256), 256)
            v = dot(r.eb[...], r.w_sb[:, at])
            r.b3s[d.co // d.cb + j, :, half_lo : half_lo + 256] = v
            r.acc[0, :, at] += rows8(v)
            r.acc[1, :, at] += rows8(v * v)

    ar_start("sk", acc_rows(2, d.co))
    weight_copy(4).wait()
    ar_mid("nb")
    norm_set("nb", ar_end("nb"), 1.0)

    inner(r.b1, r.g1, r.v2, "nb", r.w_mb, d.cb, 1)

    @pl.loop(0, d.f2)
    def _(i):
        n = i // d.t2
        base = n * d.slots + parity + 2 * (i - n * d.t2)
        for lo, hi in lanes(d.cb):
            k = taps(r.ktb, lo)
            for h in range(d.h2):
                parts = [None] * 3
                for a in range(3):
                    for b in range(3):
                        at = (2 * h + b) * d.wp
                        v = r.v2[base + a, at : at + d.wp, lo:hi].astype(F32)
                        for e in range(3):
                            p = v * k[9 * a + 3 * b + e]
                            parts[e] = p if parts[e] is None else parts[e] + p
                o = parts[1] + pltpu.roll(parts[0], 1, 0) + pltpu.roll(parts[2], d.wp - 1, 0)
                r.dz2[i, h * d.wp : (h + 1) * d.wp, lo:hi] = o

    hw = d.h2 * d.wp
    thin = one(
        lax.broadcasted_iota(jnp.int32, (d.hr, hw), 1)
        == 2 * lax.broadcasted_iota(jnp.int32, (d.hr, hw), 0)
    ).astype(BF16)

    def split(v):
        high = v.astype(BF16)
        rest = v - high.astype(F32)
        mid = rest.astype(BF16)
        return high, mid, (rest - mid.astype(F32)).astype(BF16)

    acc_clear(2, d.cb)

    @pl.loop(0, d.f2)
    def _(i):
        m = mask_o(i)
        for lo, hi in lanes(d.cb):
            v = sum(dot(thin, p) for p in split(r.dz2[i, :hw, lo:hi])) * half_cols
            r.d2[i, :, lo:hi] = v
            r.acc[0, :, lo:hi] += rows8(v) * m
            r.acc[1, :, lo:hi] += rows8(v * v) * m

    ar_start("db", acc_rows(2, d.cb))
    ar_mid("sk")
    weight_copy(5).wait()
    ar_mid("db")
    norm_set("sb", ar_end("sk"), half)
    norm_set("db", ar_end("db"), half)

    def d2_rows(ref, i, lo, hi):
        return ref[i, :, lo:hi]

    for i in range(d.f2):
        m = mask_o(i)
        for lo, hi in lanes(d.cb):
            g = activated(d2_rows(r.d2, i, lo, hi), "db", lo, hi, half_cols, m)
            r.e[i, :, lo:hi] = g
    r.g2[...] = r.e[:, :, : d.cb].reshape(d.r2, d.cb).astype(BF16)
    acc_clear(2, d.co)

    @pl.loop(0, d.co // d.cb)
    def _(j):
        for half_lo in range(0, d.cb, 256):
            at = pl.ds(pl.multiple_of(j * d.cb + half_lo, 256), 256)
            v = dot(r.g2[...], r.w_wb[:, at])
            r.b3s[j, :, half_lo : half_lo + 256] = v
            r.acc[0, :, at] += rows8(v)
            r.acc[1, :, at] += rows8(v * v)

    ar_start("wb", acc_rows(2, d.co))
    pltpu.make_async_copy(r.cotangent, r.cot, r.wsem.at[11]).wait()
    half_all = jnp.concatenate(
        [half_cols * mask_o(jnp.int32(i)) for i in range(d.f2)], axis=0
    )
    ar_mid("wb")
    norm_set("wb", ar_end("wb"), half)

    acc_clear(3, d.co)

    @pl.loop(0, d.co // LANES)
    def _(q):
        per = d.cb // LANES
        j = q // per
        at = pl.ds(pl.multiple_of((q - j * per) * LANES, LANES), LANES)
        lane = pl.ds(pl.multiple_of(q * LANES, LANES), LANES)
        i3, isk = order["wb"], order["sb"]
        b3, s = r.b3s[j, :, at], r.b3s[d.co // d.cb + j, :, at]
        z = b3 * r.par[i3, 0:1, lane] + r.par[i3, 1:2, lane]
        z = z + s * r.par[isk, 0:1, lane] + r.par[isk, 1:2, lane]
        g = logistic(z)
        y = (z * g * half_all).reshape(d.n, d.t2, d.h2, d.wh, LANES)
        sl = g * (1.0 + z * (1.0 - g)) * half_all
        for i in range(d.f2):
            n, t = i // d.t2, i % d.t2
            for h in range(d.h2):
                lo = i * d.hr + h * d.wh
                c = r.cot[n, t, h, :, lane].astype(F32)
                c = jnp.concatenate([c, jnp.zeros((d.wh - d.w2, LANES), F32)], axis=0)
                r.dz2[j, lo : lo + d.wh, at] = c * sl[lo : lo + d.wh, :]
        r.cot[:, :, :, :, lane] = y[:, :, :, : d.w2, :].astype(BF16)
        dz = r.dz2[j, :, at]
        r.acc[0, :, lane] += rows8(dz)
        r.acc[1, :, lane] += rows8(dz * b3)
        r.acc[2, :, lane] += rows8(dz * s)

    out_copy = pltpu.make_async_copy(r.cot, r.block_out, r.osem.at[0])
    out_copy.start()
    ar_start("gz", acc_rows(3, d.co))
    ar_mid("gz")
    sums = ar_end("gz")
    back_set("wb", sums[0], sums[1], half)
    back_set("sb", sums[0], sums[2], half)

    for lo in range(0, d.co, LANES):
        j, at = lo // d.cb, lo % d.cb
        dz = r.dz2[j, :, at : at + LANES]
        for name, off, dst in (("wb", 0, r.db3), ("sb", d.co // d.cb, r.ds)):
            al, be, ga = back_of(name, lo, lo + LANES)
            v = (dz * al - be - r.b3s[off + j, :, at : at + LANES] * ga) * half_all
            dst[:, lo : lo + LANES] = v.astype(BF16)

    acc_clear(2, d.cb)
    for lo, hi in lanes(d.cb, 256):
        g = dot_bt(r.db3[...], r.w_wb[lo:hi, :])
        for i in range(d.f2):
            s, b = norm_of("db", lo, hi)
            v = r.d2[i, :, lo:hi]
            dn = g[i * d.hr : (i + 1) * d.hr, :] * slope(v * s + b)
            r.dz2[i, : d.hr, lo:hi] = dn
            r.acc[0, :, lo:hi] += rows8(dn)
            r.acc[1, :, lo:hi] += rows8(dn * v)
    for n in range(d.n):
        for side, j in ((0, 0), (1, out_frames - 1)):
            at = d.r2 // 2 + n * d.hr
            r.dz2[2 * side, at : at + d.hr, :] = r.dz2[n * d.t2 + j, : d.hr, :]
            r.dz2[2 * side + 1, at : at + d.hr, :] = r.d2[n * d.t2 + j]
    ar_start("gdb", acc_rows(2, d.cb))
    halo_start(2)

    def weight_grad(name, x, y, step):
        w = getattr(r, "w_" + name)
        for lo in range(0, w.shape[1], step):
            w[:, lo : lo + step] = dot_at(x, y(lo, lo + step)).astype(BF16)
        i = WEIGHTS.index(name)
        pltpu.make_async_copy(w, getattr(r, "o_" + name), r.osem.at[1 + i]).start()

    for lo, hi in lanes(d.c0, 256):
        v = dot_bt(r.ds[...], r.w_sb[lo:hi, :])
        for i in range(d.f2):
            r.e[i, :, lo:hi] = v[i * d.hr : (i + 1) * d.hr, :]
    weight_grad("wb", r.g2[...], lambda lo, hi: r.db3[:, lo:hi], 512)
    ar_mid("gdb")
    weight_grad("sb", r.eb[...], lambda lo, hi: r.ds[:, lo:hi], 256)
    back_set("db", *ar_end("gdb"), half)

    per = d.ca // LANES
    spread = one(
        lax.broadcasted_iota(jnp.int32, (hw, d.hr), 0)
        == 2 * lax.broadcasted_iota(jnp.int32, (hw, d.hr), 1)
    ).astype(BF16)

    def u_at(slot, row, rows, lo):
        at = (lo // d.ca) * d.ur
        return (slot, slice(at + row, at + row + rows), slice(lo % d.ca, lo % d.ca + LANES))

    @pl.loop(0, d.n * d.slots)
    def _(i):
        r.u[i] = jnp.zeros((d.er, d.ca), F32)

    def grad_d2(dn, v, lo, m):
        al, be, ga = back_of("db", lo, lo + LANES)
        g = (dn * al - be - v * ga) * (half_cols * m)
        return sum(dot(spread, p) for p in split(g))

    halo_wait(2)
    for n in range(d.n):
        for lo in range(0, d.cb, LANES):
            own = [
                grad_d2(r.dz2[n * d.t2 + j, : d.hr, lo : lo + LANES], r.d2[n * d.t2 + j, :, lo : lo + LANES],
                        lo, mask_o(jnp.int32(n * d.t2 + j)))
                for j in range(d.t2)
            ]
            before = grad_d2(
                r.hr3[0, 0, n * d.hr : (n + 1) * d.hr, lo : lo + LANES], r.hr3[0, 1, n * d.hr : (n + 1) * d.hr, lo : lo + LANES], lo,
                has_prev * one(n < live) * one(parity == 1),
            )
            after = grad_d2(
                r.hr3[1, 0, n * d.hr : (n + 1) * d.hr, lo : lo + LANES], r.hr3[1, 1, n * d.hr : (n + 1) * d.hr, lo : lo + LANES], lo,
                has_next * one(n < live) * one(((start + frames) & 1) == 0),
            )
            base = n * d.slots
            r.u[u_at(base, 0, hw, lo)] = before
            for i in range(1, d.t + 2):
                v = jnp.zeros((hw, LANES), F32)
                for j in range(d.t2):
                    p = i - 1 - 2 * j
                    if p in (0, 1):
                        v = v + own[j] * one(parity == p)
                if i >= 3:
                    v = v + after * one(frames + 1 == i)
                r.u[u_at(base + i, 0, hw, lo)] = v

    acc_clear(2, d.cb)

    @pl.loop(0, d.f)
    def _(f):
        base = slot_of(f)
        m = mask_f(f)
        for lo, hi in lanes(d.cb):
            k = taps(r.ktb, lo)
            for h in range(d.h):
                rows = ((h // 2, 1),) if h % 2 == 0 else ((h // 2 + 1, 0), (h // 2, 2))
                parts = [None] * 3
                for a in range(3):
                    for row, b in rows:
                        if row >= d.h2:
                            continue
                        v = r.u[u_at(base + 1 - a, row * d.wp, d.wp, lo)]
                        for e in range(3):
                            p = v * k[9 * a + 3 * b + e]
                            parts[e] = p if parts[e] is None else parts[e] + p
                o = parts[1] + pltpu.roll(parts[0], d.wp - 1, 0) + pltpu.roll(parts[2], 1, 0)
                r.dvb[f, h * d.wp : (h + 1) * d.wp, lo:hi] = o.astype(BF16)
        for lo, hi in lanes(d.cb, 256):
            g = dot_bt(r.dvb[f], r.w_mb[lo:hi, :])
            for at in range(lo, hi, LANES):
                s, b = norm_of("nb", at, at + LANES)
                v = r.b1[f, :, at : at + LANES]
                dn = g[:, at - lo : at - lo + LANES] * slope(v * s + b) * (full_cols * m)
                r.b3s[f, :, at : at + LANES] = dn
                r.acc[0, :, at : at + LANES] += rows8(dn)
                r.acc[1, :, at : at + LANES] += rows8(dn * v)

    ar_start("gnb", acc_rows(2, d.cb))

    def shifted(v):
        return (pltpu.roll(v, d.wp - 1, 0), v, pltpu.roll(v, 1, 0))

    for lo in range(0, d.cb, LANES):
        def body(i, sums):
            n = i // d.t2
            slot = n * d.slots + parity + 2 * (i - n * d.t2)
            sums = list(sums)
            for h in range(d.h2):
                g = shifted(r.u[u_at(slot + 1, h * d.wp, d.wp, lo)] * mask_o(i))
                for a in range(3):
                    for b in range(3):
                        at = (2 * h + b) * d.wp
                        v = r.v2[slot + a, at : at + d.wp, lo : lo + LANES].astype(F32)
                        for e in range(3):
                            sums[9 * a + 3 * b + e] += rows8(v * g[e])
            return tuple(sums)

        sums = lax.fori_loop(0, d.f2, body, (jnp.zeros((8, LANES), F32),) * 27)
        for i in range(27):
            r.gkb[i : i + 1, lo : lo + LANES] = jnp.sum(sums[i], axis=0, keepdims=True)

    def flat(ref):
        return ref[...].reshape(d.f * d.fr, ref.shape[-1])

    ar_mid("gnb")
    weight_grad("mb", flat(r.g1), lambda lo, hi: r.dvb[:, :, lo:hi].reshape(d.f * d.fr, hi - lo), 256)
    back_set("nb", *ar_end("gnb"), 1.0)

    acc_clear(2, d.c0)

    @pl.loop(0, d.f)
    def _(f):
        m = mask_f(f)
        n = f // d.t
        t = f - n * d.t
        for lo, hi in lanes(d.cb):
            al, be, ga = back_of("nb", lo, hi)
            v = (r.b3s[f, :, lo:hi] * al - be - r.b1[f, :, lo:hi] * ga) * (full_cols * m)
            r.dvb[f, :, lo:hi] = v.astype(BF16)
        j = jnp.clip((t - parity) // 2, 0, d.t2 - 1)
        flag = one(((t - parity) & 1) == 0)
        for lo, hi in lanes(d.c0, 256):
            g = dot_bt(r.dvb[f], r.w_nb[lo:hi, :])
            for at in range(lo, hi, LANES):
                parts = split(r.e[n * d.t2 + j, :, at : at + LANES] * flag)
                up = sum(dot_at(pick, p) for p in parts[:2])
                z = joined(f, at, at + LANES)
                dz = (g[:, at - lo : at - lo + LANES] + up) * slope(z) * (full_cols * m)
                r.dz1[f, :, at : at + LANES] = dz.astype(BF16)
                v = r.a3[f, :, at : at + LANES].astype(F32)
                r.acc[0, :, at : at + LANES] += rows8(dz)
                r.acc[1, :, at : at + LANES] += rows8(dz * v)

    ar_start("gwa", acc_rows(2, d.c0))
    ar_mid("gwa")
    weight_grad("nb", flat(r.y1), lambda lo, hi: r.dvb[:, :, lo:hi].reshape(d.f * d.fr, hi - lo), 256)
    back_set("wa", *ar_end("gwa"), 1.0)

    acc_clear(2, d.ca)

    @pl.loop(0, d.f)
    def _(f):
        m = mask_f(f)
        for lo, hi in lanes(d.c0):
            al, be, ga = back_of("wa", lo, hi)
            v = r.dz1[f, :, lo:hi].astype(F32) * al - be - r.a3[f, :, lo:hi].astype(F32) * ga
            r.a3[f, :, lo:hi] = (v * (full_cols * m)).astype(BF16)
        g = dot_bt(r.a3[f], r.w_wa[...])
        for lo, hi in lanes(d.ca):
            s, b = norm_of("da", lo, hi)
            v = r.d1[f, :, lo:hi]
            dn = g[:, lo:hi] * slope(v * s + b)
            r.u[slot_of(f), d.wp : d.wp + d.fr, lo:hi] = dn
            r.acc[0, :, lo:hi] += rows8(dn)
            r.acc[1, :, lo:hi] += rows8(dn * v)

    halo_drain(1)
    for n in range(d.n):
        for side, k in ((0, 0), (1, frames - 1)):
            r.hs2[side, n, :, : d.ca] = r.u[n * d.slots + 1 + k, d.wp : d.wp + d.fr, :].astype(BF16)
            r.hs2[side, n, :, d.ca :] = r.d1[n * d.t + k].astype(BF16)
    ar_start("gda", acc_rows(2, d.ca))
    halo_start(3)
    ar_mid("gda")
    weight_grad("wa", flat(r.h2), lambda lo, hi: r.a3[:, :, lo:hi].reshape(d.f * d.fr, hi - lo), 256)

    @pl.loop(0, d.n * d.slots)
    def _(i):
        zero = jnp.zeros((d.wp, d.ca), F32)
        r.u[i, 0 : d.wp, :] = zero
        r.u[i, d.er - d.wp : d.er, :] = zero

    back_set("da", *ar_end("gda"), 1.0)

    def grad_d1(dn, v, lo, hi, m):
        al, be, ga = back_of("da", lo, hi)
        return (dn * al - be - v * ga) * (full_cols * m)

    mid_rows = slice(d.wp, d.wp + d.fr)

    @pl.loop(0, d.f)
    def _(f):
        m = mask_f(f)
        for lo, hi in lanes(d.ca):
            r.u[slot_of(f), mid_rows, lo:hi] = grad_d1(
                r.u[slot_of(f), mid_rows, lo:hi], r.d1[f, :, lo:hi], lo, hi, m
            )

    halo_wait(3)
    for n in range(d.n):
        for lo, hi in lanes(d.ca):
            r.u[n * d.slots, mid_rows, lo:hi] = grad_d1(
                r.hr2[0, n, :, lo:hi].astype(F32), r.hr2[0, n, :, d.ca + lo : d.ca + hi].astype(F32), lo, hi,
                has_prev * one(n < live),
            )
            v = grad_d1(
                r.hr2[1, n, :, lo:hi].astype(F32), r.hr2[1, n, :, d.ca + lo : d.ca + hi].astype(F32), lo, hi,
                has_next * one(n < live),
            )
            for k in range(1, d.t):
                at = n * d.slots + 1 + k
                r.u[at, mid_rows, lo:hi] = r.u[at, mid_rows, lo:hi] + v * one(frames == k)
            r.u[n * d.slots + 1 + d.t, mid_rows, lo:hi] = v

    halo_drain(0)
    acc_clear(2, d.ca)

    @pl.loop(0, d.f)
    def _(f):
        base = slot_of(f)
        m = mask_f(f)
        for lo, hi in lanes(d.ca):
            k = taps(r.kta, lo)
            for h in range(d.h):
                parts = [None] * 3
                for a in range(3):
                    for b in range(3):
                        v = r.u[base + 1 - a, (h + 2 - b) * d.wp : (h + 3 - b) * d.wp, lo:hi]
                        for e in range(3):
                            p = v * k[9 * a + 3 * b + e]
                            parts[e] = p if parts[e] is None else parts[e] + p
                o = parts[1] + pltpu.roll(parts[0], d.wp - 1, 0) + pltpu.roll(parts[2], 1, 0)
                r.dva[f, h * d.wp : (h + 1) * d.wp, lo:hi] = o.astype(BF16)
        g = dot_bt(r.dva[f], r.w_ma[...])
        for lo, hi in lanes(d.ca):
            s, b = norm_of("na", lo, hi)
            v = r.a1[f, :, lo:hi]
            dn = g[:, lo:hi] * slope(v * s + b) * (full_cols * m)
            r.d1[f, :, lo:hi] = dn
            r.acc[0, :, lo:hi] += rows8(dn)
            r.acc[1, :, lo:hi] += rows8(dn * v)

    ar_start("gna", acc_rows(2, d.ca))

    for lo in range(0, d.ca, LANES):
        def body(f, sums):
            slot = slot_of(f)
            m = mask_f(f)
            sums = list(sums)
            for h in range(d.h):
                g = shifted(r.u[slot, (h + 1) * d.wp : (h + 2) * d.wp, lo : lo + LANES] * m)
                for a in range(3):
                    for b in range(3):
                        at = (h + b) * d.wp
                        v = r.v1[slot - 1 + a, at : at + d.wp, lo : lo + LANES].astype(F32)
                        for e in range(3):
                            sums[9 * a + 3 * b + e] += rows8(v * g[e])
            return tuple(sums)

        sums = lax.fori_loop(0, d.f, body, (jnp.zeros((8, LANES), F32),) * 27)
        for i in range(27):
            r.gka[i : i + 1, lo : lo + LANES] = jnp.sum(sums[i], axis=0, keepdims=True)

    ar_mid("gna")
    weight_grad("ma", flat(r.h1), lambda lo, hi: r.dva[:, :, lo:hi].reshape(d.f * d.fr, hi - lo), 256)
    back_set("na", *ar_end("gna"), 1.0)

    def grad_copy(f, slot):
        return pltpu.make_async_copy(
            r.raw.at[slot], r.input_grad.at[f // d.t, f % d.t], r.isem.at[slot]
        )

    @pl.loop(0, d.f)
    def _(f):
        m = mask_f(f)
        slot = lax.rem(f, 2)
        for lo, hi in lanes(d.ca):
            al, be, ga = back_of("na", lo, hi)
            v = (r.d1[f, :, lo:hi] * al - be - r.a1[f, :, lo:hi] * ga) * (full_cols * m)
            r.dva[f, :, lo:hi] = v.astype(BF16)

        @pl.when(f >= 2)
        def _():
            grad_copy(f - 2, slot).wait()

        for lo, hi in lanes(d.c0, 256):
            g = dot_bt(r.dva[f], r.w_na[lo:hi, :]) + r.dz1[f, :, lo:hi].astype(F32)
            g = g.astype(BF16).reshape(d.h, d.wp, hi - lo)
            r.raw[slot, :, :, lo:hi] = g[:, : d.w, :]
        grad_copy(f, slot).start()

    weight_grad("na", flat2(r.x, d), lambda lo, hi: r.dva[:, :, lo:hi].reshape(d.f * d.fr, hi - lo), 256)
    for i, (src, dst) in enumerate(((r.small, r.o_small), (r.gka, r.o_gka), (r.gkb, r.o_gkb))):
        pltpu.make_async_copy(src, dst, r.osem.at[8 + i]).start()

    grad_copy(d.f - 2, d.f % 2).wait()
    grad_copy(d.f - 1, (d.f - 1) % 2).wait()
    out_copy.wait()
    for i, name in enumerate(WEIGHTS):
        pltpu.make_async_copy(getattr(r, "w_" + name), getattr(r, "o_" + name), r.osem.at[1 + i]).wait()
    for i, (src, dst) in enumerate(((r.small, r.o_small), (r.gka, r.o_gka), (r.gkb, r.o_gkb))):
        pltpu.make_async_copy(src, dst, r.osem.at[8 + i]).wait()
    for name in msgs:
        ar_drain(name)
    for i in (2, 3):
        halo_drain(i)


def flat2(ref, d):
    return ref[...].reshape(d.f * d.fr, d.c0)


def per_device(mesh, *args):
    (
        clip_in, cotangent, frame_count, clip_count, narrow_a, narrow_gain_a, narrow_bias_a, mixing_a,
        depthwise_a, depth_gain_a, depth_bias_a, widen_a, widen_gain_a, widen_bias_a, narrow_b,
        narrow_gain_b, narrow_bias_b, mixing_b, depthwise_b, depth_gain_b, depth_bias_b, widen_b,
        widen_gain_b, widen_bias_b, shortcut_b, shortcut_gain_b, shortcut_bias_b,
    ) = args
    d = Dims(mesh, clip_in.shape, cotangent.shape, narrow_a.shape[1], narrow_b.shape[1])
    vectors = (
        narrow_gain_a, narrow_bias_a, depth_gain_a, depth_bias_a, widen_gain_a, widen_bias_a,
        narrow_gain_b, narrow_bias_b, depth_gain_b, depth_bias_b, widen_gain_b, widen_bias_b,
        shortcut_gain_b, shortcut_bias_b,
    )
    packed = jnp.stack([jnp.pad(v, (0, d.co - v.shape[0])) for v in vectors] + [jnp.zeros((d.co,), F32)] * 2)

    def taps_of(k):
        return jnp.pad(k.astype(F32).T, ((0, 5), (0, 0)))

    scratch = scratch_of(d)
    names = INPUTS + OUTPUTS + tuple(scratch)
    shapes = dict(
        block_out=jax.ShapeDtypeStruct(cotangent.shape, BF16),
        input_grad=jax.ShapeDtypeStruct(clip_in.shape, BF16),
        o_small=jax.ShapeDtypeStruct((16, d.co), F32),
        o_gka=jax.ShapeDtypeStruct((32, d.ca), F32),
        o_gkb=jax.ShapeDtypeStruct((32, d.cb), F32),
        o_na=jax.ShapeDtypeStruct(narrow_a.shape, BF16),
        o_ma=jax.ShapeDtypeStruct(mixing_a.shape, BF16),
        o_wa=jax.ShapeDtypeStruct(widen_a.shape, BF16),
        o_nb=jax.ShapeDtypeStruct(narrow_b.shape, BF16),
        o_mb=jax.ShapeDtypeStruct(mixing_b.shape, BF16),
        o_wb=jax.ShapeDtypeStruct(widen_b.shape, BF16),
        o_sb=jax.ShapeDtypeStruct(shortcut_b.shape, BF16),
    )
    anywhere = pl.BlockSpec(memory_space=pl.ANY)
    scalars = pl.BlockSpec(memory_space=pltpu.SMEM)
    outs = pl.pallas_call(
        functools.partial(kernel, d, names),
        out_shape=[shapes[name] for name in OUTPUTS],
        in_specs=[scalars if name.endswith("_count") else anywhere for name in INPUTS],
        out_specs=[anywhere] * len(OUTPUTS),
        scratch_shapes=list(scratch.values()),
        compiler_params=pltpu.CompilerParams(
            collective_id=0, has_side_effects=True, vmem_limit_bytes=63 * 1024 * 1024
        ),
    )(
        clip_in, cotangent, frame_count, clip_count, narrow_a, mixing_a, widen_a, narrow_b, mixing_b,
        widen_b, shortcut_b, taps_of(depthwise_a), taps_of(depthwise_b), packed,
    )
    out = dict(zip(OUTPUTS, outs))

    def share(g):
        part = lax.psum_scatter(g.astype(BF16), "tm", scatter_dimension=0, tiled=True)
        return lax.psum(part, "clip").astype(F32)

    def share_taps(g):
        return share(g[:27].T)

    small = out["o_small"]
    grads = [small[i, : v.shape[0]] for i, v in enumerate(vectors)]
    return (
        out["block_out"], out["input_grad"],
        share(out["o_na"]), grads[0], grads[1], share(out["o_ma"]), share_taps(out["o_gka"]),
        grads[2], grads[3], share(out["o_wa"]), grads[4], grads[5],
        share(out["o_nb"]), grads[6], grads[7], share(out["o_mb"]), share_taps(out["o_gkb"]),
        grads[8], grads[9], share(out["o_wb"]), grads[10], grads[11],
        share(out["o_sb"]), grads[12], grads[13],
    )


def solution(mesh):
    data = P("clip", "tm", None, None, None)
    rows = P("tm", None)
    in_specs = (data, data, P(), P("clip")) + (P(),) * 23
    block = (rows, P(), P(), rows, rows, P(), P(), rows, P(), P())
    out_specs = (data, data) + block + block + (rows, P(), P())
    return jax.shard_map(
        functools.partial(per_device, mesh), mesh=mesh, in_specs=in_specs, out_specs=out_specs,
        check_vma=False,
    )
```

profile of v0, /device:TPU:0, one launch (start us, length us, event | category | flops | bytes accessed | tf_op | source)
XLA Modules:
  0.0 562.5 jit_solution(6931642814319829416)
XLA Ops:
  17.5 2.3 copy.58.refs_1_
  19.8 5.0 copy.57.refs_0_
  24.9 1.4 stack.63.refs_13_
  26.3 156.6 %shard_map.450 = (bf16[2,2,7,7,2048]{4,3,2,1,0:T(8,128)(2,1)}, bf16[2,4,14,14,1024]{4,3,2,1,0:T(8,128)(2,1)}, f32[16,2048]{1,0:T(8,128)}, f32[32,256]{1,0:T(8,12...) custom-call(bf16[2,4,14,14,1024]{4,3,2,1,0:T(8,128)(2,1)} %copy.57.r, ...), custom_call_target="tpu_custom_call" | custom-call | tf_op jit(solution)/shard_map/pallas_call | solution.py:1069
  188.9 1.8 copy.59
  190.7 6.7 %copy.60 = bf16[2,4,14,14,1024]{4,1,3,2,0:T(4,128)(2,1)} copy(bf16[2,4,14,14,1024]{4,3,2,1,0:T(8,128)(2,1)} %get-tuple-element.75) | data formatting | bytes 6422528
  197.4 15.7 %reduce-scatter.14.cloned.1.call-done = bf16[128,256]{1,0:T(8,128)(2,1)} async-done(((bf16[1024,256]{1,0:T(8,128)(2,1)}), bf16[128,256]{1,0:T(8,128)(2,1)}) %reduce-scatter.14.cloned.1.call-update) | async-done | bytes 65552 | tf_op jit(solution)/shard_map/reduce_scatter | solution.py:1085
  213.2 31.5 %reduce-scatter.18.cloned.1.call-done = bf16[32,1024]{1,0:T(8,128)(2,1)} async-done(((bf16[256,1024]{1,0:T(8,128)(2,1)}), bf16[32,1024]{1,0:T(8,128)(2,1)}) %reduce-scatter.18.cloned.1.call-update) | async-done | bytes 65552 | tf_op jit(solution)/shard_map/reduce_scatter | solution.py:1085
  244.6 31.4 %reduce-scatter.22.cloned.1.call-done = bf16[64,512]{1,0:T(8,128)(2,1)} async-done(((bf16[512,512]{1,0:T(8,128)(2,1)}), bf16[64,512]{1,0:T(8,128)(2,1)}) %reduce-scatter.22.cloned.1.call-update) | async-done | bytes 65552 | tf_op jit(solution)/shard_map/reduce_scatter | solution.py:1085
  276.1 32.8 %reduce-scatter.20.cloned.1.call-done = bf16[128,512]{1,0:T(8,128)(2,1)} async-done(((bf16[1024,512]{1,0:T(8,128)(2,1)}), bf16[128,512]{1,0:T(8,128)(2,1)}) %reduce-scatter.20.cloned.1.call-update) | async-done | bytes 131088 | tf_op jit(solution)/shard_map/reduce_scatter | solution.py:1085
  308.8 36.3 %reduce-scatter.24.cloned.1.call-done = bf16[64,2048]{1,0:T(8,128)(2,1)} async-done(((bf16[512,2048]{1,0:T(8,128)(2,1)}), bf16[64,2048]{1,0:T(8,128)(2,1)}) %reduce-scatter.24.cloned.1.call-update) | async-done | bytes 262160 | tf_op jit(solution)/shard_map/reduce_scatter | solution.py:1085
  345.2 50.9 %reduce-scatter.26.cloned.1.call-done = bf16[128,2048]{1,0:T(8,128)(2,1)} async-done(((bf16[1024,2048]{1,0:T(8,128)(2,1)}), bf16[128,2048]{1,0:T(8,128)(2,1)}) %reduce-scatter.26.cloned.1.call-update) | async-done | bytes 524304 | tf_op jit(solution)/shard_map/reduce_scatter | solution.py:1085
  400.3 1.6 fusion.2
  402.0 25.2 %reduce-scatter.28.cloned.1.call-done = bf16[32,27]{1,0:T(8,128)(2,1)} async-done(((bf16[256,27]{1,0:T(8,128)(2,1)}), bf16[32,27]{1,0:T(8,128)(2,1)}) %reduce-scatter.28.cloned.1.call-update) | async-done | bytes 1744
  427.9 30.3 %reduce-scatter.30.cloned.1.call-done = bf16[64,27]{1,0:T(8,128)(2,1)} async-done(((bf16[512,27]{1,0:T(8,128)(2,1)}), bf16[64,27]{1,0:T(8,128)(2,1)}) %reduce-scatter.30.cloned.1.call-update) | async-done | bytes 3472
  459.1 29.8 %reduce-scatter.16.cloned.1.call-done = bf16[32,256]{1,0:T(8,128)(2,1)} async-done(((bf16[256,256]{1,0:T(8,128)(2,1)}), bf16[32,256]{1,0:T(8,128)(2,1)}) %reduce-scatter.16.cloned.1.call-update) | async-done | bytes 16400 | tf_op jit(solution)/shard_map/reduce_scatter | solution.py:1085
  488.9 16.5 %all-reduce.12 = (bf16[32,27]{0,1:T(8,128)(2,1)S(1)}, bf16[32,256]{1,0:T(8,128)(2,1)S(1)}, bf16[64,27]{0,1:T(8,128)(2,1)S(1)}) all-reduce(bf16[32,27]{0,1:T(8,128)(2,1)S(1)} %copy.63, bf16[32,256]{1,0:T(8,128)(2,1)} %reduce-scatter.16.cloned.1.call-done, bf16[64,27]{0,1:T(8,128)(2,1)S(1)} %copy.65), channel_id=1, replica_groups=mesh['clip'=4,'tm'=8] {'clip'}, use_global_device_ids=true, to_apply=%region_5.6 | all-reduce | flops 10784 | bytes 43136 | tf_op jit(solution)/shard_map/psum | solution.py:1086
  507.3 38.3 %all-reduce.16.cloned.1.call-done = (bf16[128,256]{1,0:T(8,128)(2,1)}, bf16[32,1024]{1,0:T(8,128)(2,1)}, bf16[128,512]{1,0:T(8,128)(2,1)}, bf16[64,512]{1,0:T(8,...) async-done(((bf16[128,256]{1,0:T(8,128)(2,1)}, bf16[32,1024]{1,0:T(8,128)(2,1)}, bf16[128,512]{1,0:T(8,128)(2,1)}, bf16[64,512]{1,0:T(8,128)(2,1)}, ...) | async-done | bytes 1114128 | tf_op jit(solution)/shard_map/psum | solution.py:1086
  545.6 1.5 convert_element_type.54
  547.1 1.5 convert_element_type.58
  548.6 1.5 convert_element_type.60
  550.1 1.6 convert_element_type.59
  551.8 1.8 convert_element_type.63
  553.5 2.1 convert_element_type.64
  (59 shorter events, 23.2 us)
Async XLA Ops:
  7.2 206.0 %reduce-scatter.14.cloned.1.call-start = ((), (), s32[]{:S(2)}) async-start(), calls=%async_computation.9 | async-start | bytes 589824 | tf_op jit(solution)/shard_map/reduce_scatter | solution.py:1085
  19.8 5.0 copy-start.2
  19.8 5.0 copy-start.3
  19.8 5.0 copy-start.4
  19.8 5.0 copy-start.5
  182.9 61.7 %reduce-scatter.18.cloned.1.call-start = ((), (), s32[]{:S(2)}) async-start(), calls=%async_computation.11 | async-start | bytes 589824 | tf_op jit(solution)/shard_map/reduce_scatter | solution.py:1085
  183.7 92.4 %reduce-scatter.22.cloned.1.call-start = ((), (), s32[]{:S(2)}) async-start(), calls=%async_computation.13 | async-start | bytes 589824 | tf_op jit(solution)/shard_map/reduce_scatter | solution.py:1085
  184.4 124.5 %reduce-scatter.20.cloned.1.call-start = ((), (), s32[]{:S(2)}) async-start(), calls=%async_computation.12 | async-start | bytes 1179648 | tf_op jit(solution)/shard_map/reduce_scatter | solution.py:1085
  184.4 1.8 copy-start.6
  184.4 2.6 copy-start.1
  185.0 3.9 copy-start
  185.0 160.2 %reduce-scatter.24.cloned.1.call-start = ((), (), s32[]{:S(2)}) async-start(), calls=%async_computation.14 | async-start | bytes 2359296 | tf_op jit(solution)/shard_map/reduce_scatter | solution.py:1085
  185.6 210.5 %reduce-scatter.26.cloned.1.call-start = ((), (), s32[]{:S(2)}) async-start(), calls=%async_computation.15 | async-start | bytes 4718592 | tf_op jit(solution)/shard_map/reduce_scatter | solution.py:1085
  186.1 241.0 %reduce-scatter.28.cloned.1.call-start = ((), (), s32[]{:S(2)}) async-start(), calls=%async_computation.16 | async-start | bytes 73728
  187.0 271.3 %reduce-scatter.30.cloned.1.call-start = ((), (), s32[]{:S(2)}) async-start(), calls=%async_computation.17 | async-start | bytes 147456
  187.9 301.0 %reduce-scatter.16.cloned.1.call-start = ((), (), s32[]{:S(2)}) async-start(), calls=%async_computation.10 | async-start | bytes 147456 | tf_op jit(solution)/shard_map/reduce_scatter | solution.py:1085
  188.6 357.0 %all-reduce.16.cloned.1.call-start = ((), (), s32[]{:S(2)}) async-start(), calls=%async_computation.18 | async-start | bytes 2228224 | tf_op jit(solution)/shard_map/psum | solution.py:1086
Sparse Core Ops, SparseCore 0:
  183.0 30.0 reduce-scatter.13
  215.5 29.0 reduce-scatter.17
  246.9 29.1 reduce-scatter.21
  278.3 30.4 reduce-scatter.19
  311.1 34.0 reduce-scatter.23
  347.4 48.5 reduce-scatter.25
  398.9 28.1 reduce-scatter.27
  430.0 28.2 reduce-scatter.29
  460.6 28.2 reduce-scatter.15
  492.5 53.0 all-reduce.15
where the time goes:
time: 564 us; the launch traced here: 562 us
  waiting for transfers between devices  326 us (58%)
  Pallas kernels  157 us (28%)
  local copies, waits for them, and re-layouts  33.9 us (6%)
  blocking collectives  16.5 us (3%)
  between operations  15 us (3%)
  other arithmetic  14 us (2%)
    reduce_scatter x7, waiting for transfers between devices, share(): lax.psum_scatter(g.astype(BF16), 'tm', scatter_dimension=0, tiled=True)  228 us
    pallas_call x1, Pallas kernels, per_device(): pl.pallas_call(functools.partial(kernel, d, names), out_shape=[shapes[nam...  157 us
    unnamed x12, waiting for transfers between devices  59.2 us
    psum x1, waiting for transfers between devices, share(): return lax.psum(part, 'clip').astype(F32)  38.3 us
    unnamed x23, local copies, waits for them, and re-layouts  19.7 us
    psum x1, blocking collectives, share(): return lax.psum(part, 'clip').astype(F32)  16.5 us
  transfers between devices with their start and end apart: 10, of which 10 were waited for; matrix products, arithmetic and copies ran while one was open for 3% of the time, Pallas kernels for 0%

commit v1 on v0

--- a/solution.py
+++ b/solution.py
@@ -56,6 +56,41 @@
     if width == v.shape[1]:
         return v
     return jnp.concatenate([v] * (width // v.shape[1]), axis=1)
+
+
+class Piece:
+    def __init__(self, d, name, weight, rows, lo, hi, first, split):
+        self.name, self.weight, self.lo, self.hi = name, weight, lo, hi
+        self.n, self.rb = hi - lo, rows // d.nt
+        self.first, self.split = first, split
+        self.shape1 = self.cut((self.rb, self.n), split[0])
+        self.shape2 = self.cut(self.shape1, split[1])
+
+    @staticmethod
+    def cut(shape, axis):
+        return (shape[0] // 2, shape[1]) if axis == "r" else (shape[0], shape[1] // 2)
+
+    def window(self, level, bit):
+        rows, cols = self.shape1 if level == 1 else self.shape2
+        if self.split[level - 1] == "r":
+            at = bit * rows
+            return (pl.ds(at if isinstance(at, int) else pl.multiple_of(at, rows), rows), slice(None))
+        at = bit * cols
+        return (slice(None), pl.ds(at if isinstance(at, int) else pl.multiple_of(at, cols), cols))
+
+
+def pieces_of(d):
+    half = d.co // 2
+    return [
+        Piece(d, "wb", "wb", d.cb, 0, d.co, "x", "rr"),
+        Piece(d, "sb0", "sb", d.c0, 0, half, "y", "rr"),
+        Piece(d, "sb1", "sb", d.c0, half, d.co, "x", "rr"),
+        Piece(d, "nb", "nb", d.c0, 0, d.cb, "y", "rr"),
+        Piece(d, "mb", "mb", d.cb, 0, d.cb, "x", "rr"),
+        Piece(d, "wa", "wa", d.ca, 0, d.c0, "y", "cc"),
+        Piece(d, "na", "na", d.c0, 0, d.ca, "x", "rr"),
+        Piece(d, "ma", "ma", d.ca, 0, d.ca, "y", "cr"),
+    ]
 
 
 class Dims:
@@ -78,13 +113,16 @@
         self.hr = self.h2 * self.wh
         self.r2 = self.f2 * self.hr
         self.ur = (self.h2 + 1) * self.wp
+        self.staged = self.nt == 8 and self.nc == 4
+        self.nz = self.nt // 2
+        self.pieces = pieces_of(self) if self.staged else []
 
 
 def messages(d):
     return dict(
         na=(3, d.ca), da=(2, d.ca), wa=(2, d.c0), nb=(2, d.cb), sk=(2, d.co), db=(2, d.cb),
         wb=(2, d.co), gz=(3, d.co), gdb=(2, d.cb), gnb=(2, d.cb), gwa=(2, d.c0), gda=(2, d.ca),
-        gna=(2, d.ca),
+        gna=(2, d.ca), ka=(32, d.ca), kb=(32, d.cb),
     )
 
 
@@ -92,16 +130,15 @@
     V = pltpu.VMEM
     DM = pltpu.SemaphoreType.DMA
     s = dict(
-        raw=V((2, d.h, d.w, d.c0), BF16),
-        x=V((d.f, d.h, d.wp, d.c0), BF16),
-        a1=V((d.f, d.fr, d.ca), F32),
+        x=V((d.f, d.fr, d.c0), BF16),
+        a1=V((d.f, d.fr, d.ca), BF16),
         h1=V((d.f, d.fr, d.ca), BF16),
         v1=V((d.n * d.slots, d.er, d.ca), BF16),
         d1=V((d.f, d.fr, d.ca), F32),
         h2=V((d.f, d.fr, d.ca), BF16),
         a3=V((d.f, d.fr, d.c0), BF16),
         y1=V((d.f, d.fr, d.c0), BF16),
-        b1=V((d.f, d.fr, d.cb), F32),
+        b1=V((d.f, d.fr, d.cb), BF16),
         g1=V((d.f, d.fr, d.cb), BF16),
         v2=V((d.n * d.slots, d.er, d.cb), BF16),
         d2=V((d.f2, d.hr, d.cb), F32),
@@ -114,9 +151,7 @@
         ds=V((d.r2, d.co), BF16),
         u=V((d.n * d.slots, d.er, d.ca), F32),
         dvb=V((d.f, d.fr, d.cb), BF16),
-        dz1=V((d.f, d.fr, d.c0), BF16),
         dva=V((max(d.f, 4 * d.n), d.fr, d.ca), BF16),
-        cot=V((d.n, d.t2, d.h2, d.w2, d.co), BF16),
         acc=V((3, 8, d.co), F32),
         inv=V((1, d.co), F32),
         kta=V((32, d.ca), F32),
@@ -139,15 +174,24 @@
         w_sb=V((d.c0, d.co), BF16),
         small=V((16, d.co), F32),
         wsem=DM((16,)),
-        xsem=DM((2,)),
-        osem=DM((16,)),
-        isem=DM((2,)),
+        xsem=DM((d.f,)),
+        osem=DM((24,)),
+        gsem=DM((8, 4)),
+        isem=DM((d.f,)),
     )
     for name, (k, c) in messages(d).items():
+        kind = BF16 if k == 32 else F32
         for p, (_, _, size) in enumerate(d.phases):
-            s[f"ms{p}_{name}"] = V((k, c), F32)
-            s[f"ml{p}_{name}"] = V((size, k, c), F32)
+            s[f"ms{p}_{name}"] = V((k, c), kind)
+            s[f"ml{p}_{name}"] = V((size, k, c), kind)
         s["mq_" + name] = DM((len(d.phases), 2))
+    for p in d.pieces:
+        s["gs_" + p.name] = DM((5, 2))
+        s["gc_" + p.name] = V((d.nz, p.rb, p.n), BF16)
+        s["g1_" + p.name] = V((d.nz,) + p.shape1, BF16)
+        s["g2_" + p.name] = V((d.nz,) + p.shape2, BF16)
+        s["g3_" + p.name] = V((d.nz,) + p.shape2, BF16)
+        s["g4_" + p.name] = V((d.nc,) + p.shape2, BF16)
     return s
 
 
@@ -176,14 +220,15 @@
             getattr(r, "i_" + name), getattr(r, "w_" + name), r.wsem.at[i]
         )
 
-    def frame_copy(f, slot):
-        return pltpu.make_async_copy(r.clip_in.at[f // d.t, f % d.t], r.raw.at[slot], r.xsem.at[slot])
-
-    frame_copy(0, 0).start()
+    def frame_copy(f):
+        return pltpu.make_async_copy(r.clip_in.at[f], r.x.at[f], r.xsem.at[f])
+
+    frame_copy(0).start()
     weight_copy(0).start()
-    frame_copy(1, 1).start()
+    for f in range(1, d.f):
+        frame_copy(f).start()
     for i, (src, dst) in enumerate(
-        ((r.i_kta, r.kta), (r.i_ktb, r.ktb), (r.i_vec, r.vec), (r.cotangent, r.cot))
+        ((r.i_kta, r.kta), (r.i_ktb, r.ktb), (r.i_vec, r.vec), (r.cotangent, r.ds))
     ):
         pltpu.make_async_copy(src, dst, r.wsem.at[8 + i]).start()
     for i in range(1, len(WEIGHTS)):
@@ -234,7 +279,7 @@
     def ar_send(name, p, value):
         src, slots = getattr(r, f"ms{p}_{name}"), getattr(r, f"ml{p}_{name}")
         q = getattr(r, "mq_" + name)
-        src[...] = value
+        src[...] = value.astype(src.dtype)
 
         @pl.loop(1, d.phases[p][2])
         def _(k):
@@ -243,7 +288,7 @@
                 device_id_type=MESH,
             ).start()
 
-        slots[place(p)] = value
+        slots[place(p)] = value.astype(src.dtype)
 
     def ar_wait(name, p, which):
         part = getattr(r, f"ml{p}_{name}").at[pl.ds(0, d.phases[p][2] - 1)]
@@ -251,7 +296,7 @@
 
     def ar_total(name, p):
         ar_wait(name, p, 1)
-        return jnp.sum(getattr(r, f"ml{p}_{name}")[...], axis=0)
+        return jnp.sum(getattr(r, f"ml{p}_{name}")[...].astype(F32), axis=0)
 
     def ar_start(name, rows):
         ar_send(name, 0, jnp.concatenate(rows, axis=0))
@@ -262,11 +307,132 @@
 
     def ar_end(name):
         total = ar_total(name, last)
+        if msgs[name][0] == 32:
+            return total
         return [total[i : i + 1, :] for i in range(msgs[name][0])]
 
     def ar_drain(name):
         for p in range(last + 1):
             ar_wait(name, p, 0)
+
+    core, zed = lax.rem(tm, 2), tm // 2
+    bit = dict(x=lax.rem(clip, 2), y=clip // 2)
+    step = dict(x=1 - 2 * bit["x"], y=2 - 4 * bit["y"])
+
+    def block(p, i):
+        if p.weight in ("na", "nb"):
+            per = d.er // p.rb
+            ref = r.v1 if p.weight == "na" else r.v2
+            return ref.at[i // per, pl.ds(pl.multiple_of(lax.rem(i, per) * p.rb, p.rb), p.rb), :]
+        return getattr(r, "w_" + p.weight).at[pl.ds(pl.multiple_of(i * p.rb, p.rb), p.rb), p.lo : p.hi]
+
+    def bits(p):
+        return (bit["x"], bit["y"]) if p.first == "x" else (bit["y"], bit["x"])
+
+    def stage_copy(p, stage, src, dst, clip_at, tm_at):
+        q = getattr(r, "gs_" + p.name)
+        return pltpu.make_async_remote_copy(
+            src, dst, q.at[stage, 0], q.at[stage, 1], device_id=(clip_at, tm_at), device_id_type=MESH
+        )
+
+    def stage_ref(p, stage):
+        part = getattr(r, ("gc_", "g1_", "g2_", "g3_", "g4_")[stage] + p.name)
+        return part if stage < 3 else part.at[pl.ds(0, part.shape[0] - 1)]
+
+    def stage_wait(p, stage, which):
+        part = stage_ref(p, stage)
+        pltpu.make_async_copy(part, part, getattr(r, "gs_" + p.name).at[stage, which]).wait()
+
+    def add(dst, src):
+        dst[...] = (dst[...].astype(F32) + src[...].astype(F32)).astype(BF16)
+
+    def stage0(p):
+        land = getattr(r, "gc_" + p.name)
+        for z in range(d.nz):
+            stage_copy(p, 0, block(p, 2 * z + 1 - core), land.at[z], clip, tm + 1 - 2 * core).start()
+
+    def stage1(p):
+        stage_wait(p, 0, 1)
+        here, land = getattr(r, "gc_" + p.name), getattr(r, "g1_" + p.name)
+        for z in range(d.nz):
+            add(here.at[z], block(p, 2 * z + core))
+        b = bits(p)[0]
+        src = here.at[(slice(None),) + p.window(1, 1 - b)]
+        stage_copy(p, 1, src, land, clip + step[p.first], tm).start()
+
+    def stage2(p):
+        stage_wait(p, 1, 1)
+        before, here, land = (getattr(r, q + p.name) for q in ("gc_", "g1_", "g2_"))
+        b = bits(p)
+        for z in range(d.nz):
+            add(here.at[z], before.at[(z,) + p.window(1, b[0])])
+        src = here.at[(slice(None),) + p.window(2, 1 - b[1])]
+        stage_copy(p, 2, src, land, clip + step["y" if p.first == "x" else "x"], tm).start()
+
+    def stage3(p):
+        stage_wait(p, 2, 1)
+        before, here, land = (getattr(r, q + p.name) for q in ("g1_", "g2_", "g3_"))
+        b = bits(p)
+        for z in range(d.nz):
+            add(here.at[z], before.at[(z,) + p.window(2, b[1])])
+        for k in range(1, d.nz):
+            z = lax.rem(zed + k, d.nz)
+            stage_copy(p, 3, here.at[z], land.at[zed], clip, 2 * z + core).start()
+        land[zed] = here[zed]
+
+    def stage4(p):
+        stage_wait(p, 3, 1)
+        here, land = getattr(r, "g3_" + p.name), getattr(r, "g4_" + p.name)
+        land[clip] = jnp.sum(here[...].astype(F32), axis=0).astype(BF16)
+        for k in range(1, d.nc):
+            at = lax.rem(clip + k, d.nc)
+            stage_copy(p, 4, land.at[clip], land.at[clip], at, tm).start()
+
+    slab = dict(sb0=(0, 0), sb1=(2, 0), wb=(0, 128), nb=(4, 0), mb=(5, 0), wa=(6, 0), na=(5, 64), ma=(7, 64))
+
+    def out_copies(p):
+        j, row = slab[p.name]
+        out = getattr(r, "o_" + p.weight)
+        wide = min(p.n, d.cb)
+        i = [q.name for q in d.pieces].index(p.name)
+        return [
+            pltpu.make_async_copy(
+                r.b3s.at[j + c, row : row + p.rb, :wide],
+                out.at[:, p.lo + c * wide : p.lo + (c + 1) * wide],
+                r.gsem.at[i, c],
+            )
+            for c in range(p.n // wide)
+        ]
+
+    def stage5(p):
+        stage_wait(p, 4, 1)
+        land = getattr(r, "g4_" + p.name)
+        j, row = slab[p.name]
+        rows, cols = p.shape2
+        for q in range(d.nc):
+            b = (q % 2, q // 2) if p.first == "x" else (q // 2, q % 2)
+            at = [0, 0]
+            size = [p.rb, p.n]
+            for axis, one_bit in zip(p.split, b):
+                k = 0 if axis == "r" else 1
+                size[k] //= 2
+                at[k] += one_bit * size[k]
+            for lo in range(0, cols, min(cols, d.cb)):
+                col = at[1] + lo
+                r.b3s[
+                    j + col // d.cb, row + at[0] : row + at[0] + rows,
+                    col % d.cb : col % d.cb + min(cols, d.cb),
+                ] = land[q, :, lo : lo + min(cols, d.cb)].astype(F32)
+        for copy in out_copies(p):
+            copy.start()
+
+    named = {p.name: p for p in d.pieces}
+    stages = (stage0, stage1, stage2, stage3, stage4, stage5)
+
+    def send(stage, *pieces):
+        for name in pieces:
+            if d.staged:
+                stages[stage](named[name])
 
     def halo_source(i, side):
         src = getattr(r, HALO[i][0])
@@ -381,24 +547,16 @@
 
     @pl.loop(0, d.f)
     def _(f):
-        slot = lax.rem(f, 2)
-        frame_copy(f, slot).wait()
-        r.x[f] = jnp.zeros((d.h, d.wp, d.c0), BF16)
-        r.x[f, :, 0 : d.w, :] = r.raw[slot]
-
-        @pl.when(f + 2 < d.f)
-        def _():
-            frame_copy(f + 2, slot).start()
-
-        v = dot(r.x[f].reshape(d.fr, d.c0), r.w_na[...])
-        r.a1[f] = v
+        frame_copy(f).wait()
+        v = dot(r.x[f], r.w_na[...])
+        r.a1[f] = v.astype(BF16)
         m = mask_f(f)
         r.acc[0, :, : d.ca] += rows8(v) * m
         r.acc[1, :, : d.ca] += rows8(v * v) * m
 
     for n in range(d.n):
-        r.dva[n] = r.a1[n * d.t].astype(BF16)
-        r.dva[d.n + n] = r.a1[n * d.t + frames - 1].astype(BF16)
+        r.dva[n] = r.a1[n * d.t]
+        r.dva[d.n + n] = r.a1[n * d.t + frames - 1]
     pl.semaphore_wait(barrier, sum(size - 1 for _, _, size in d.phases))
     cells = (jnp.minimum(live, d.n) * frames * (d.h * d.w)).astype(F32)
     ar_start("na", acc_rows(2, d.ca) + [jnp.full((1, d.ca), 1.0, F32) * cells])
@@ -436,7 +594,7 @@
         def _(f):
             m = mask_f(f)
             for lo, hi in lanes(c):
-                hid[f, :, lo:hi] = activated(ref_in[f, :, lo:hi], name, lo, hi, cols, m).astype(BF16)
+                hid[f, :, lo:hi] = activated(ref_in[f, :, lo:hi].astype(F32), name, lo, hi, cols, m).astype(BF16)
             framed[slot_of(f), d.wp : d.wp + d.fr, :] = mixed(hid[f], weight[...]).astype(framed.dtype)
 
         halo_wait(half_i)
@@ -518,7 +676,7 @@
 
     def joined(f, lo, hi):
         s, b = norm_of("wa", lo, hi)
-        x = r.x[f, :, :, lo:hi].reshape(d.fr, hi - lo).astype(F32)
+        x = r.x[f, :, lo:hi].astype(F32)
         return r.a3[f, :, lo:hi].astype(F32) * s + b + x
 
     acc_clear(2, d.cb)
@@ -530,13 +688,13 @@
             r.y1[f, :, lo:hi] = (silu(joined(f, lo, hi)) * (full_cols * m)).astype(BF16)
         for lo, hi in lanes(d.cb, 256):
             v = dot(r.y1[f], r.w_nb[:, lo:hi])
-            r.b1[f, :, lo:hi] = v
+            r.b1[f, :, lo:hi] = v.astype(BF16)
             r.acc[0, :, lo:hi] += rows8(v)
             r.acc[1, :, lo:hi] += rows8(v * v)
 
     for n in range(d.n):
-        r.hs2[0, n] = r.b1[n * d.t].astype(BF16)
-        r.hs2[1, n] = r.b1[n * d.t + frames - 1].astype(BF16)
+        r.hs2[0, n] = r.b1[n * d.t]
+        r.hs2[1, n] = r.b1[n * d.t + frames - 1]
     ar_start("nb", acc_rows(2, d.cb))
     halo_start(1)
 
@@ -642,7 +800,7 @@
             r.acc[1, :, at] += rows8(v * v)
 
     ar_start("wb", acc_rows(2, d.co))
-    pltpu.make_async_copy(r.cotangent, r.cot, r.wsem.at[11]).wait()
+    pltpu.make_async_copy(r.cotangent, r.ds, r.wsem.at[11]).wait()
     half_all = jnp.concatenate(
         [half_cols * mask_o(jnp.int32(i)) for i in range(d.f2)], axis=0
     )
@@ -662,22 +820,15 @@
         z = b3 * r.par[i3, 0:1, lane] + r.par[i3, 1:2, lane]
         z = z + s * r.par[isk, 0:1, lane] + r.par[isk, 1:2, lane]
         g = logistic(z)
-        y = (z * g * half_all).reshape(d.n, d.t2, d.h2, d.wh, LANES)
+        r.db3[:, lane] = (z * g * half_all).astype(BF16)
         sl = g * (1.0 + z * (1.0 - g)) * half_all
-        for i in range(d.f2):
-            n, t = i // d.t2, i % d.t2
-            for h in range(d.h2):
-                lo = i * d.hr + h * d.wh
-                c = r.cot[n, t, h, :, lane].astype(F32)
-                c = jnp.concatenate([c, jnp.zeros((d.wh - d.w2, LANES), F32)], axis=0)
-                r.dz2[j, lo : lo + d.wh, at] = c * sl[lo : lo + d.wh, :]
-        r.cot[:, :, :, :, lane] = y[:, :, :, : d.w2, :].astype(BF16)
-        dz = r.dz2[j, :, at]
+        dz = r.ds[:, lane].astype(F32) * sl
+        r.dz2[j, :, at] = dz
         r.acc[0, :, lane] += rows8(dz)
         r.acc[1, :, lane] += rows8(dz * b3)
         r.acc[2, :, lane] += rows8(dz * s)
 
-    out_copy = pltpu.make_async_copy(r.cot, r.block_out, r.osem.at[0])
+    out_copy = pltpu.make_async_copy(r.db3, r.block_out, r.osem.at[0])
     out_copy.start()
     ar_start("gz", acc_rows(3, d.co))
     ar_mid("gz")
@@ -685,6 +836,7 @@
     back_set("wb", sums[0], sums[1], half)
     back_set("sb", sums[0], sums[2], half)
 
+    out_copy.wait()
     for lo in range(0, d.co, LANES):
         j, at = lo // d.cb, lo % d.cb
         dz = r.dz2[j, :, at : at + LANES]
@@ -711,20 +863,22 @@
     ar_start("gdb", acc_rows(2, d.cb))
     halo_start(2)
 
-    def weight_grad(name, x, y, step):
+    def weight_grad(name, x, y, step, lo=0, hi=None):
         w = getattr(r, "w_" + name)
-        for lo in range(0, w.shape[1], step):
-            w[:, lo : lo + step] = dot_at(x, y(lo, lo + step)).astype(BF16)
-        i = WEIGHTS.index(name)
-        pltpu.make_async_copy(w, getattr(r, "o_" + name), r.osem.at[1 + i]).start()
+        for at in range(lo, hi or w.shape[1], step):
+            w[:, at : at + step] = dot_at(x, y(at, at + step)).astype(BF16)
 
     for lo, hi in lanes(d.c0, 256):
         v = dot_bt(r.ds[...], r.w_sb[lo:hi, :])
         for i in range(d.f2):
             r.e[i, :, lo:hi] = v[i * d.hr : (i + 1) * d.hr, :]
     weight_grad("wb", r.g2[...], lambda lo, hi: r.db3[:, lo:hi], 512)
+    send(0, "wb")
     ar_mid("gdb")
-    weight_grad("sb", r.eb[...], lambda lo, hi: r.ds[:, lo:hi], 256)
+    weight_grad("sb", r.eb[...], lambda lo, hi: r.ds[:, lo:hi], 256, 0, d.co // 2)
+    send(0, "sb0")
+    weight_grad("sb", r.eb[...], lambda lo, hi: r.ds[:, lo:hi], 256, d.co // 2, d.co)
+    send(0, "sb1")
     back_set("db", *ar_end("gdb"), half)
 
     per = d.ca // LANES
@@ -799,13 +953,14 @@
             g = dot_bt(r.dvb[f], r.w_mb[lo:hi, :])
             for at in range(lo, hi, LANES):
                 s, b = norm_of("nb", at, at + LANES)
-                v = r.b1[f, :, at : at + LANES]
+                v = r.b1[f, :, at : at + LANES].astype(F32)
                 dn = g[:, at - lo : at - lo + LANES] * slope(v * s + b) * (full_cols * m)
                 r.b3s[f, :, at : at + LANES] = dn
                 r.acc[0, :, at : at + LANES] += rows8(dn)
                 r.acc[1, :, at : at + LANES] += rows8(dn * v)
 
     ar_start("gnb", acc_rows(2, d.cb))
+    send(1, "wb", "sb0", "sb1")
 
     def shifted(v):
         return (pltpu.roll(v, d.wp - 1, 0), v, pltpu.roll(v, 1, 0))
@@ -832,8 +987,10 @@
     def flat(ref):
         return ref[...].reshape(d.f * d.fr, ref.shape[-1])
 
+    ar_start("kb", [r.gkb[...]])
     ar_mid("gnb")
     weight_grad("mb", flat(r.g1), lambda lo, hi: r.dvb[:, :, lo:hi].reshape(d.f * d.fr, hi - lo), 256)
+    send(0, "mb")
     back_set("nb", *ar_end("gnb"), 1.0)
 
     acc_clear(2, d.c0)
@@ -845,8 +1002,21 @@
         t = f - n * d.t
         for lo, hi in lanes(d.cb):
             al, be, ga = back_of("nb", lo, hi)
-            v = (r.b3s[f, :, lo:hi] * al - be - r.b1[f, :, lo:hi] * ga) * (full_cols * m)
+            v = (r.b3s[f, :, lo:hi] * al - be - r.b1[f, :, lo:hi].astype(F32) * ga) * (full_cols * m)
             r.dvb[f, :, lo:hi] = v.astype(BF16)
+
+    for i in range(0, d.c0, d.er):
+        for lo, hi in lanes(d.cb, 256):
+            x = r.y1[:, :, i : i + d.er].reshape(d.f * d.fr, d.er)
+            y = r.dvb[:, :, lo:hi].reshape(d.f * d.fr, hi - lo)
+            r.v2[i // d.er, :, lo:hi] = dot_at(x, y).astype(BF16)
+    send(0, "nb")
+
+    @pl.loop(0, d.f)
+    def _(f):
+        m = mask_f(f)
+        n = f // d.t
+        t = f - n * d.t
         j = jnp.clip((t - parity) // 2, 0, d.t2 - 1)
         flag = one(((t - parity) & 1) == 0)
         for lo, hi in lanes(d.c0, 256):
@@ -856,14 +1026,16 @@
                 up = sum(dot_at(pick, p) for p in parts[:2])
                 z = joined(f, at, at + LANES)
                 dz = (g[:, at - lo : at - lo + LANES] + up) * slope(z) * (full_cols * m)
-                r.dz1[f, :, at : at + LANES] = dz.astype(BF16)
+                r.y1[f, :, at : at + LANES] = dz.astype(BF16)
                 v = r.a3[f, :, at : at + LANES].astype(F32)
                 r.acc[0, :, at : at + LANES] += rows8(dz)
                 r.acc[1, :, at : at + LANES] += rows8(dz * v)
 
     ar_start("gwa", acc_rows(2, d.c0))
+    send(2, "wb", "sb0", "sb1")
+    ar_mid("kb")
     ar_mid("gwa")
-    weight_grad("nb", flat(r.y1), lambda lo, hi: r.dvb[:, :, lo:hi].reshape(d.f * d.fr, hi - lo), 256)
+    send(1, "mb", "nb")
     back_set("wa", *ar_end("gwa"), 1.0)
 
     acc_clear(2, d.ca)
@@ -873,7 +1045,7 @@
         m = mask_f(f)
         for lo, hi in lanes(d.c0):
             al, be, ga = back_of("wa", lo, hi)
-            v = r.dz1[f, :, lo:hi].astype(F32) * al - be - r.a3[f, :, lo:hi].astype(F32) * ga
+            v = r.y1[f, :, lo:hi].astype(F32) * al - be - r.a3[f, :, lo:hi].astype(F32) * ga
             r.a3[f, :, lo:hi] = (v * (full_cols * m)).astype(BF16)
         g = dot_bt(r.a3[f], r.w_wa[...])
         for lo, hi in lanes(d.ca):
@@ -891,8 +1063,11 @@
             r.hs2[side, n, :, d.ca :] = r.d1[n * d.t + k].astype(BF16)
     ar_start("gda", acc_rows(2, d.ca))
     halo_start(3)
+    send(3, "wb", "sb0", "sb1")
     ar_mid("gda")
+    send(2, "mb", "nb")
     weight_grad("wa", flat(r.h2), lambda lo, hi: r.a3[:, :, lo:hi].reshape(d.f * d.fr, hi - lo), 256)
+    send(0, "wa")
 
     @pl.loop(0, d.n * d.slots)
     def _(i):
@@ -954,13 +1129,16 @@
         g = dot_bt(r.dva[f], r.w_ma[...])
         for lo, hi in lanes(d.ca):
             s, b = norm_of("na", lo, hi)
-            v = r.a1[f, :, lo:hi]
+            v = r.a1[f, :, lo:hi].astype(F32)
             dn = g[:, lo:hi] * slope(v * s + b) * (full_cols * m)
             r.d1[f, :, lo:hi] = dn
             r.acc[0, :, lo:hi] += rows8(dn)
             r.acc[1, :, lo:hi] += rows8(dn * v)
 
     ar_start("gna", acc_rows(2, d.ca))
+    send(4, "wb", "sb0", "sb1")
+    send(3, "mb", "nb")
+    send(1, "wa")
 
     for lo in range(0, d.ca, LANES):
         def body(f, sums):
@@ -981,53 +1159,79 @@
         for i in range(27):
             r.gka[i : i + 1, lo : lo + LANES] = jnp.sum(sums[i], axis=0, keepdims=True)
 
+    ar_start("ka", [r.gka[...]])
     ar_mid("gna")
-    weight_grad("ma", flat(r.h1), lambda lo, hi: r.dva[:, :, lo:hi].reshape(d.f * d.fr, hi - lo), 256)
+    weight_grad("ma", flat(r.h1), lambda lo, hi: r.dva[: d.f, :, lo:hi].reshape(d.f * d.fr, hi - lo), 256)
+    send(0, "ma")
     back_set("na", *ar_end("gna"), 1.0)
 
-    def grad_copy(f, slot):
-        return pltpu.make_async_copy(
-            r.raw.at[slot], r.input_grad.at[f // d.t, f % d.t], r.isem.at[slot]
-        )
+    def grad_copy(f):
+        return pltpu.make_async_copy(r.y1.at[f], r.input_grad.at[f], r.isem.at[f])
 
     @pl.loop(0, d.f)
     def _(f):
         m = mask_f(f)
-        slot = lax.rem(f, 2)
         for lo, hi in lanes(d.ca):
             al, be, ga = back_of("na", lo, hi)
-            v = (r.d1[f, :, lo:hi] * al - be - r.a1[f, :, lo:hi] * ga) * (full_cols * m)
+            v = (r.d1[f, :, lo:hi] * al - be - r.a1[f, :, lo:hi].astype(F32) * ga) * (full_cols * m)
             r.dva[f, :, lo:hi] = v.astype(BF16)
 
-        @pl.when(f >= 2)
-        def _():
-            grad_copy(f - 2, slot).wait()
-
+    x = r.x[...].reshape(d.f * d.fr, d.c0)
+    y = r.dva[: d.f].reshape(d.f * d.fr, d.ca)
+    for i in range(0, d.c0, d.er):
+        r.v1[i // d.er] = dot_at(x[:, i : i + d.er], y).astype(BF16)
+    send(0, "na")
+    send(2, "wa")
+    send(4, "mb", "nb")
+    send(1, "ma")
+    send(5, "wb", "sb0", "sb1")
+    ar_mid("ka")
+
+    @pl.loop(0, d.f)
+    def _(f):
         for lo, hi in lanes(d.c0, 256):
-            g = dot_bt(r.dva[f], r.w_na[lo:hi, :]) + r.dz1[f, :, lo:hi].astype(F32)
-            g = g.astype(BF16).reshape(d.h, d.wp, hi - lo)
-            r.raw[slot, :, :, lo:hi] = g[:, : d.w, :]
-        grad_copy(f, slot).start()
-
-    weight_grad("na", flat2(r.x, d), lambda lo, hi: r.dva[:, :, lo:hi].reshape(d.f * d.fr, hi - lo), 256)
-    for i, (src, dst) in enumerate(((r.small, r.o_small), (r.gka, r.o_gka), (r.gkb, r.o_gkb))):
-        pltpu.make_async_copy(src, dst, r.osem.at[8 + i]).start()
-
-    grad_copy(d.f - 2, d.f % 2).wait()
-    grad_copy(d.f - 1, (d.f - 1) % 2).wait()
-    out_copy.wait()
-    for i, name in enumerate(WEIGHTS):
-        pltpu.make_async_copy(getattr(r, "w_" + name), getattr(r, "o_" + name), r.osem.at[1 + i]).wait()
-    for i, (src, dst) in enumerate(((r.small, r.o_small), (r.gka, r.o_gka), (r.gkb, r.o_gkb))):
-        pltpu.make_async_copy(src, dst, r.osem.at[8 + i]).wait()
+            g = dot_bt(r.dva[f], r.w_na[lo:hi, :]) + r.y1[f, :, lo:hi].astype(F32)
+            r.y1[f, :, lo:hi] = g.astype(BF16)
+        grad_copy(f).start()
+
+    send(1, "na")
+    send(3, "wa")
+    send(2, "ma")
+    send(5, "mb", "nb")
+    send(2, "na")
+    send(4, "wa")
+    send(3, "ma")
+    r.gka[...] = ar_end("ka")
+    r.gkb[...] = ar_end("kb")
+    tail = [(r.small, r.o_small), (r.gka, r.o_gka), (r.gkb, r.o_gkb)]
+    send(3, "na")
+    send(4, "ma")
+    send(5, "wa")
+    send(4, "na")
+    send(5, "ma")
+    send(5, "na")
+    if not d.staged:
+        tail += [(getattr(r, "w_" + n), getattr(r, "o_" + n)) for n in ("ma", "wa", "mb", "wb", "sb")]
+        for ref, out, rows, cols in ((r.v1, r.o_na, d.c0, d.ca), (r.v2, r.o_nb, d.c0, d.cb)):
+            for i in range(0, rows, d.er):
+                tail.append((ref.at[i // d.er], out.at[i : i + d.er, :]))
+    tail = [pltpu.make_async_copy(src, dst, r.osem.at[1 + i]) for i, (src, dst) in enumerate(tail)]
+    for copy in tail:
+        copy.start()
+
+    for f in range(d.f):
+        grad_copy(f).wait()
+    for copy in tail:
+        copy.wait()
+    for p in d.pieces:
+        for copy in out_copies(p):
+            copy.wait()
+        for stage in range(5):
+            stage_wait(p, stage, 0)
     for name in msgs:
         ar_drain(name)
     for i in (2, 3):
         halo_drain(i)
-
-
-def flat2(ref, d):
-    return ref[...].reshape(d.f * d.fr, d.c0)
 
 
 def per_device(mesh, *args):
@@ -1045,24 +1249,32 @@
     )
     packed = jnp.stack([jnp.pad(v, (0, d.co - v.shape[0])) for v in vectors] + [jnp.zeros((d.co,), F32)] * 2)
 
+    def columns(v, width):
+        return jnp.pad(v, ((0, 0),) * 3 + ((0, width - v.shape[3]), (0, 0)))
+
     def taps_of(k):
         return jnp.pad(k.astype(F32).T, ((0, 5), (0, 0)))
 
     scratch = scratch_of(d)
     names = INPUTS + OUTPUTS + tuple(scratch)
+    def grad_shape(w):
+        if d.staged:
+            return jax.ShapeDtypeStruct((w.shape[0] // d.nt, w.shape[1]), F32)
+        return jax.ShapeDtypeStruct(w.shape, BF16)
+
     shapes = dict(
-        block_out=jax.ShapeDtypeStruct(cotangent.shape, BF16),
-        input_grad=jax.ShapeDtypeStruct(clip_in.shape, BF16),
+        block_out=jax.ShapeDtypeStruct((d.r2, d.co), BF16),
+        input_grad=jax.ShapeDtypeStruct((d.f, d.fr, d.c0), BF16),
         o_small=jax.ShapeDtypeStruct((16, d.co), F32),
         o_gka=jax.ShapeDtypeStruct((32, d.ca), F32),
         o_gkb=jax.ShapeDtypeStruct((32, d.cb), F32),
-        o_na=jax.ShapeDtypeStruct(narrow_a.shape, BF16),
-        o_ma=jax.ShapeDtypeStruct(mixing_a.shape, BF16),
-        o_wa=jax.ShapeDtypeStruct(widen_a.shape, BF16),
-        o_nb=jax.ShapeDtypeStruct(narrow_b.shape, BF16),
-        o_mb=jax.ShapeDtypeStruct(mixing_b.shape, BF16),
-        o_wb=jax.ShapeDtypeStruct(widen_b.shape, BF16),
-        o_sb=jax.ShapeDtypeStruct(shortcut_b.shape, BF16),
+        o_na=grad_shape(narrow_a),
+        o_ma=grad_shape(mixing_a),
+        o_wa=grad_shape(widen_a),
+        o_nb=grad_shape(narrow_b),
+        o_mb=grad_shape(mixing_b),
+        o_wb=grad_shape(widen_b),
+        o_sb=grad_shape(shortcut_b),
     )
     anywhere = pl.BlockSpec(memory_space=pl.ANY)
     scalars = pl.BlockSpec(memory_space=pltpu.SMEM)
@@ -1073,25 +1285,32 @@
         out_specs=[anywhere] * len(OUTPUTS),
         scratch_shapes=list(scratch.values()),
         compiler_params=pltpu.CompilerParams(
-            collective_id=0, has_side_effects=True, vmem_limit_bytes=63 * 1024 * 1024
+            collective_id=0, has_side_effects=True, vmem_limit_bytes=65200 * 1024
         ),
     )(
-        clip_in, cotangent, frame_count, clip_count, narrow_a, mixing_a, widen_a, narrow_b, mixing_b,
+        columns(clip_in, d.wp).reshape(d.f, d.fr, d.c0),
+        columns(cotangent, d.wh).reshape(d.r2, d.co), frame_count, clip_count, narrow_a, mixing_a, widen_a, narrow_b, mixing_b,
         widen_b, shortcut_b, taps_of(depthwise_a), taps_of(depthwise_b), packed,
     )
     out = dict(zip(OUTPUTS, outs))
 
     def share(g):
+        if d.staged:
+            return g
         part = lax.psum_scatter(g.astype(BF16), "tm", scatter_dimension=0, tiled=True)
         return lax.psum(part, "clip").astype(F32)
 
+    tm = lax.axis_index("tm")
+
     def share_taps(g):
-        return share(g[:27].T)
+        rows = g.shape[1] // d.nt
+        return lax.dynamic_slice_in_dim(g[:27], tm * rows, rows, 1).T
 
     small = out["o_small"]
     grads = [small[i, : v.shape[0]] for i, v in enumerate(vectors)]
     return (
-        out["block_out"], out["input_grad"],
+        out["block_out"].reshape(d.n, d.t2, d.h2, d.wh, d.co)[:, :, :, : d.w2],
+        out["input_grad"].reshape(d.n, d.t, d.h, d.wp, d.c0)[:, :, :, : d.w],
         share(out["o_na"]), grads[0], grads[1], share(out["o_ma"]), share_taps(out["o_gka"]),
         grads[2], grads[3], share(out["o_wa"]), grads[4], grads[5],
         share(out["o_nb"]), grads[6], grads[7], share(out["o_mb"]), share_taps(out["o_gkb"]),

time: 564 us -> 245 us (0.43)
  waiting for transfers between devices: 326 us -> 0 us
  Pallas kernels: 157 us -> 211 us
  blocking collectives: 16.5 us -> 0 us
  between operations: 15 us -> 1.69 us
  other arithmetic: 14 us -> 1.25 us
    reduce_scatter x7 -> x0, waiting for transfers between devices: 228 us -> none  [share(): lax.psum_scatter(g.astype(BF16), 'tm', scatter_dimension=0, tiled=True)]
    unnamed x12 -> x0, waiting for transfers between devices: 59.2 us -> none
    pallas_call x1, Pallas kernels: 157 us -> 211 us  [per_device(): pl.pallas_call(functools.partial(kernel, d, names), out_shape=[shapes[nam...]
    psum x1 -> x0, waiting for transfers between devices: 38.3 us -> none  [share(): return lax.psum(part, 'clip').astype(F32)]
    psum x1 -> x0, blocking collectives: 16.5 us -> none  [share(): return lax.psum(part, 'clip').astype(F32)]
    convert_element_type x8 -> x0, other arithmetic: 11.3 us -> none  [share(): return lax.psum(part, 'clip').astype(F32)]
    pad x10, local copies, waits for them, and re-layouts: 6.84 us -> 0.04 us  [per_device(): jnp.pad(v, (0, d.co - v.shape[0]))]
    unnamed x23 -> x62, local copies, waits for them, and re-layouts: 19.7 us -> 17.8 us
  transfers between devices with their start and end apart: 10 -> 0, of which waited for: 10 -> 0; matrix products, arithmetic and copies ran while one was open for 3% -> 0% of each run, Pallas kernels for 0% -> 0%
where the time goes in v1:
time: 245 us
  Pallas kernels  211 us (86%)
  local copies, waits for them, and re-layouts  31.1 us (13%)
    pallas_call x1, Pallas kernels, per_device(): pl.pallas_call(functools.partial(kernel, d, names), out_shape=[shapes[nam...  211 us
    unnamed x62, local copies, waits for them, and re-layouts  17.8 us
    slice x4, local copies, waits for them, and re-layouts, per_device(): grads = [small[i, :v.shape[0]] for i, v in enumerate(vectors)]  5.86 us

profile of v1, /device:TPU:0, one launch (start us, length us, event | category | flops | bytes accessed | tf_op | source)
XLA Modules:
  0.0 244.8 jit_solution(13520894712158266021)
XLA Ops:
  0.7 3.1 %copy.59 = bf16[2,4,14,14,1024]{4,3,2,1,0:T(8,128)(2,1)S(1)} copy(bf16[2,4,14,14,1024]{4,1,3,2,0:T(4,128)(2,1)} %param.27) | data formatting | bytes 6422528
  3.8 2.6 %pad.53.clone = bf16[2,4,14,16,1024]{4,3,2,1,0:T(8,128)(2,1)} pad(bf16[2,4,14,14,1024]{4,3,2,1,0:T(8,128)(2,1)S(1)} %copy.59, bf16[]{:T(256)} %constant.4.clone.1), padding=0_0x0_0x0_0x0_2x0_0 | pad | bytes 6881282 | tf_op jit(solution)/shard_map/jit(_pad)/pad | solution.py:1253
  6.5 0.3 copy.60
  6.8 1.1 pad.54.clone
  8.1 1.4 stack.63.refs_13_
  9.6 0.6 pad_convert_fusion.refs_12_
  10.2 0.6 pad_convert_fusion.1.refs_11_
  11.5 210.8 %shard_map.450 = (bf16[224,2048]{1,0:T(8,128)(2,1)}, bf16[8,224,1024]{2,1,0:T(8,128)(2,1)}, f32[16,2048]{1,0:T(8,128)}, f32[32,256]{1,0:T(8,128)}, f32[32,512]{1...) custom-call(bf16[8,224,1024]{2,1,0:T(8,128)(2,1)} %bitcast.42, ...), custom_call_target="tpu_custom_call" | custom-call | tf_op jit(solution)/shard_map/pallas_call | solution.py:1281
  222.3 0.9 dynamic-slice_bitcast_fusion.1
  223.2 0.7 copy.56
  223.9 1.4 dynamic-slice_bitcast_fusion
  225.3 1.6 fusion
  226.9 1.4 fusion.1
  228.3 1.4 fusion.3
  229.7 1.4 fusion.2
  231.2 6.8 %copy.58 = bf16[2,4,14,14,1024]{4,1,3,2,0:T(4,128)(2,1)} copy(bf16[2,4,14,14,1024]{4,3,2,1,0:T(8,128)(2,1)} %bitcast.43) | data formatting | bytes 6422528
  238.0 1.8 copy.57
  239.8 0.7 copy.69
  240.4 0.6 copy.70
  241.1 0.7 copy.71
  241.7 0.7 copy.72
  242.4 0.7 copy.73
  243.1 0.8 copy.74
  243.9 1.0 copy.75
  (61 shorter events, 0.2 us)
Async XLA Ops:
  3.7 2.7 %copy-start.2 = (bf16[2,2,7,7,2048]{4,1,3,2,0:T(2,128)(2,1)S(1)}, bf16[2,2,7,7,2048]{4,1,3,2,0:T(2,128)(2,1)}, u32[]{:S(2)}) copy-start(bf16[2,2,7,7,2048]{4,1,3,2,0:T(2,128)(2,1)} %param.28) | copy-start | bytes 2408452
  3.7 4.1 %copy-start.17 = (f32[512]{0:T(512)S(1)}, f32[512]{0:T(512)}, u32[]{:S(2)}) copy-start(f32[512]{0:T(512)} %param.42) | copy-start | bytes 6148
  3.8 4.1 %copy-start.18 = (f32[512]{0:T(512)S(1)}, f32[512]{0:T(512)}, u32[]{:S(2)}) copy-start(f32[512]{0:T(512)} %param.43) | copy-start | bytes 6148
  3.8 4.1 %copy-start.19 = (f32[512]{0:T(512)S(1)}, f32[512]{0:T(512)}, u32[]{:S(2)}) copy-start(f32[512]{0:T(512)} %param.46) | copy-start | bytes 6148
  3.8 4.1 %copy-start.20 = (f32[512]{0:T(512)S(1)}, f32[512]{0:T(512)}, u32[]{:S(2)}) copy-start(f32[512]{0:T(512)} %param.47) | copy-start | bytes 6148
  3.8 4.1 %copy-start.21 = (f32[256]{0:T(256)S(1)}, f32[256]{0:T(256)}, u32[]{:S(2)}) copy-start(f32[256]{0:T(256)} %param.32) | copy-start | bytes 3076
  3.8 4.2 %copy-start.22 = (f32[256]{0:T(256)S(1)}, f32[256]{0:T(256)}, u32[]{:S(2)}) copy-start(f32[256]{0:T(256)} %param.33) | copy-start | bytes 3076
  3.8 4.2 %copy-start.23 = (f32[256]{0:T(256)S(1)}, f32[256]{0:T(256)}, u32[]{:S(2)}) copy-start(f32[256]{0:T(256)} %param.36) | copy-start | bytes 3076
  3.8 4.2 %copy-start.24 = (f32[256]{0:T(256)S(1)}, f32[256]{0:T(256)}, u32[]{:S(2)}) copy-start(f32[256]{0:T(256)} %param.37) | copy-start | bytes 3076
  3.8 4.2 %copy-start.15 = (f32[1024]{0:T(1024)S(1)}, f32[1024]{0:T(1024)}, u32[]{:S(2)}) copy-start(f32[1024]{0:T(1024)} %param.39) | copy-start | bytes 12292
  6.4 1.7 copy-start.11
  6.4 1.7 copy-start.12
  6.4 1.7 copy-start.13
  6.4 1.7 copy-start.14
  6.4 3.1 %copy-start.8 = (bf16[512,27]{0,1:T(8,128)(2,1)S(1)}, bf16[512,27]{0,1:T(8,128)(2,1)}, u32[]{:S(2)}) copy-start(bf16[512,27]{0,1:T(8,128)(2,1)} %param.45) | copy-start | bytes 82948
  6.4 3.8 %copy-start.10 = (bf16[256,27]{0,1:T(8,128)(2,1)S(1)}, bf16[256,27]{0,1:T(8,128)(2,1)}, u32[]{:S(2)}) copy-start(bf16[256,27]{0,1:T(8,128)(2,1)} %param.35) | copy-start | bytes 41476
  222.3 15.7 %copy-start.1 = (bf16[224,2048]{1,0:T(8,128)(2,1)S(1)}, bf16[224,2048]{1,0:T(8,128)(2,1)}, u32[]{:S(2)}) copy-start(bf16[224,2048]{1,0:T(8,128)(2,1)} %get-tuple-element.37) | copy-start | bytes 2752516
  231.1 8.6 %copy-start.7 = (f32[128,256]{1,0:T(8,128)S(1)}, f32[128,256]{1,0:T(8,128)}, u32[]{:S(2)}) copy-start(f32[128,256]{1,0:T(8,128)} %get-tuple-element.115) | copy-start | bytes 393220
  231.1 9.3 %copy-start.9 = (f32[32,256]{1,0:T(8,128)S(1)}, f32[32,256]{1,0:T(8,128)}, u32[]{:S(2)}) copy-start(f32[32,256]{1,0:T(8,128)} %get-tuple-element.118) | copy-start | bytes 98308
  231.1 9.9 %copy-start.6 = (f32[32,1024]{1,0:T(8,128)S(1)}, f32[32,1024]{1,0:T(8,128)}, u32[]{:S(2)}) copy-start(f32[32,1024]{1,0:T(8,128)} %get-tuple-element.122) | copy-start | bytes 393220
  231.1 10.6 %copy-start.4 = (f32[128,512]{1,0:T(8,128)S(1)}, f32[128,512]{1,0:T(8,128)}, u32[]{:S(2)}) copy-start(f32[128,512]{1,0:T(8,128)} %get-tuple-element.125) | copy-start | bytes 786436
  231.2 11.3 %copy-start.5 = (f32[64,512]{1,0:T(8,128)S(1)}, f32[64,512]{1,0:T(8,128)}, u32[]{:S(2)}) copy-start(f32[64,512]{1,0:T(8,128)} %get-tuple-element.128) | copy-start | bytes 393220
  231.2 11.9 %copy-start.3 = (f32[64,2048]{1,0:T(8,128)S(1)}, f32[64,2048]{1,0:T(8,128)}, u32[]{:S(2)}) copy-start(f32[64,2048]{1,0:T(8,128)} %get-tuple-element.132) | copy-start | bytes 1572868
  238.0 5.9 %copy-start = (f32[128,2048]{1,0:T(8,128)S(1)}, f32[128,2048]{1,0:T(8,128)}, u32[]{:S(2)}) copy-start(f32[128,2048]{1,0:T(8,128)} %get-tuple-element.135) | copy-start | bytes 3145732
  (1 other events, 1.6 us)
